TPU v7x, 32 devices: a whole 2x2x4 slice. The times are simulated.
32 devices in a mesh: dp: 16 (over z, y, x), tensor: 2 (over core).
Axes of the slice: x: 2, y: 2, z: 4, core: 2. Of those that a mesh axis runs over, the one named last changes fastest.
Arguments:
- tokens: bfloat16 [8192, 768], P('dp'), may hold values from -6 to 6
- segment_ids: int32 [16, 512], P('dp'), may hold values from 0 to 7, never falling along the last dimension, each value on 1 to 256 neighbouring positions
- expert_ids: int32 [8192, 2], P('dp'), may hold values from 0 to 3, all different within a row
- slot_order: int32 [16, 1024], P('dp'), may hold values from 0 to 1023, each once within a row
- gain_attn: bfloat16 [768], P('dp'), may hold values from 0.5 to 1.5
- qkv_weight: bfloat16 [768, 3, 768], P('dp', None, 'tensor'), may hold values from -0.21875 to 0.21875
- out_weight: bfloat16 [768, 768], P('tensor', 'dp'), may hold values from -0.625 to 0.625
- gain_ffn: bfloat16 [768], P('dp'), may hold values from 0.5 to 1.5
- router_weight: bfloat16 [768, 4], P('dp'), may hold values from -0.15625 to 0.15625
- gate_up: bfloat16 [4, 768, 2, 2048], P(None, 'dp', None, 'tensor'), may hold values from -0.21875 to 0.21875
- down_weight: bfloat16 [4, 2048, 768], P(None, 'tensor', 'dp'), may hold values from -0.25 to 0.25
- shared_gate_up: bfloat16 [768, 2, 2048], P('dp', None, 'tensor'), may hold values from -0.21875 to 0.21875
- shared_down: bfloat16 [2048, 768], P('tensor', 'dp'), may hold values from -0.1875 to 0.1875
- cotangent: bfloat16 [8192, 768], P('dp'), may hold values from -6 to 6
Outputs:
- output: bfloat16 [8192, 768], P('dp')
- grad_tokens: float32 [8192, 768], P('dp')
- grad_gain_attn: float32 [768], P('dp')
- grad_qkv: float32 [768, 3, 768], P('dp', None, 'tensor')
- grad_out: float32 [768, 768], P('tensor', 'dp')
- grad_gain_ffn: float32 [768], P('dp')
- grad_router: float32 [768, 4], P('dp')
- grad_gate_up: float32 [4, 768, 2, 2048], P(None, 'dp', None, 'tensor')
- grad_down: float32 [4, 2048, 768], P(None, 'tensor', 'dp')
- grad_shared_gate_up: float32 [768, 2, 2048], P('dp', None, 'tensor')
- grad_shared_down: float32 [2048, 768], P('tensor', 'dp')
Inputs may be any that keep to these rules, and one draw needn't show every extreme that they name: `segment_ids`: in each row segment numbers never fall; each document has 1 to 256 tokens and one has exactly that many. `expert_ids`: each row names 2 different experts. Each row is a permutation of the 1024 pairs' ranks; pair t * 2 + r of the sequence has rank slot_order[t * 2 + r].
All inputs are finite; a program needn't handle non-finite values.
Results may differ from a plain program's by a relative error of at most 0.015.
Values may be sent and summed in bfloat16 or wider, within the bound.
A program may use at most 192 MiB of HBM per device.

v0:
```python
import math

import jax
import jax.numpy as jnp
from jax import lax
from jax.sharding import PartitionSpec as P

HD = 64


epsilon = 1e-06


def rms_scale(values):
    return lax.rsqrt(jnp.mean(values * values, axis=-1, keepdims=True) + epsilon)


def rotary(length, head_dim):
    half_dim = head_dim // 2
    position = jnp.arange(length).astype(jnp.float32)[:, None]
    inverse = jnp.exp(
        jnp.arange(half_dim).astype(jnp.float32) * (-2.0 * math.log(10000.0) / head_dim)
    )
    angles = position * inverse[None, :]
    return (jnp.cos(angles)[:, None, :], jnp.sin(angles)[:, None, :])


def rotate(values, cosine, sine):
    half_dim = values.shape[-1] // 2
    first_half = values[..., :half_dim]
    second_half = values[..., half_dim:]
    return jnp.concatenate(
        [first_half * cosine - second_half * sine, second_half * cosine + first_half * sine],
        axis=-1,
    )


def route_slots(pair_ids, rank_order, capacity, experts):
    length = pair_ids.shape[0]
    top_count = pair_ids.shape[1]
    pair_expert = pair_ids.reshape(-1)
    pair_count = pair_expert.shape[0]
    ordered = jnp.zeros((pair_count,), jnp.int32).at[rank_order].set(pair_expert)
    onehot = (ordered[:, None] == jnp.arange(experts, dtype=jnp.int32)[None, :]).astype(jnp.int32)
    running = jnp.cumsum(onehot, axis=0)
    ranked_slot = jnp.sum(running * onehot, axis=1) - 1
    position = ranked_slot[rank_order]
    kept_pair = position < capacity
    slot_index = jnp.where(kept_pair, pair_expert * capacity + position, experts * capacity)
    token_of_pair = jnp.arange(pair_count, dtype=jnp.int32) // top_count
    slot_token = (
        jnp.full((experts * capacity,), length, jnp.int32)
        .at[slot_index]
        .set(token_of_pair, mode="drop")
    )
    return (slot_token, slot_index.reshape(length, top_count), kept_pair.reshape(length, top_count))


def silu_back(both_parts, grad_hidden):
    gate_part = both_parts[..., 0, :]
    up_part = both_parts[..., 1, :]
    sigma = jax.nn.sigmoid(gate_part)
    slope = sigma * (1.0 + gate_part * (1.0 - sigma))
    return jnp.stack(
        [grad_hidden * up_part * slope, grad_hidden * gate_part * sigma], axis=-2
    ).astype(jnp.bfloat16)


def silu_forward(both_parts):
    return (jax.nn.silu(both_parts[..., 0, :]) * both_parts[..., 1, :]).astype(jnp.bfloat16)


def norm_back(grad_norm, values, scale_rows, gain):
    grad_gain = jnp.sum(grad_norm * values * scale_rows, axis=0)
    inner = grad_norm * gain
    grad_values = scale_rows * inner - values * scale_rows**3 * jnp.mean(
        inner * values, axis=-1, keepdims=True
    )
    return (grad_values, grad_gain)


def split_blocks(length):
    block = min(512, length)
    return (block, length // block)


def masked_scores(query_block, keys_all, query_pos, query_seg, segment, scale):
    positions = jnp.arange(keys_all.shape[0])
    scores = (
        jnp.einsum("qhd,khd->hqk", query_block, keys_all, preferred_element_type=jnp.float32)
        * scale
    )
    allowed = (positions[None, :] <= query_pos[:, None]) & (segment[None, :] == query_seg[:, None])
    return jnp.where(allowed[None], scores, -1e30)


def attend_forward(queries, keys_all, values_all, segment, scale):
    length, head_count, head_dim = queries.shape
    block, count_blocks = split_blocks(length)
    positions = jnp.arange(length)

    def one_block(inputs):
        query_block, query_pos, query_seg = inputs
        scores = masked_scores(query_block, keys_all, query_pos, query_seg, segment, scale)
        largest = jnp.max(scores, axis=-1, keepdims=True)
        expo = jnp.exp(scores - largest)
        total = jnp.sum(expo, axis=-1, keepdims=True)
        probs = (expo / total).astype(jnp.bfloat16)
        mixed = jnp.einsum("hqk,khd->qhd", probs, values_all, preferred_element_type=jnp.float32)
        return (mixed.astype(jnp.bfloat16), (largest + jnp.log(total))[..., 0])

    blocks = (
        queries.reshape(count_blocks, block, head_count, head_dim),
        positions.reshape(count_blocks, block),
        segment.reshape(count_blocks, block),
    )
    mixed_all, log_totals = lax.map(one_block, blocks)
    return (mixed_all.reshape(length, head_count * head_dim), log_totals)


def attend_backward(queries, keys_all, values_all, segment, scale, grad_mixed, log_totals):
    length, head_count, head_dim = queries.shape
    block, count_blocks = split_blocks(length)
    positions = jnp.arange(length)

    def one_block(carry, inputs):
        grad_keys, grad_values = carry
        query_block, query_pos, query_seg, grad_block, log_block = inputs
        scores = masked_scores(query_block, keys_all, query_pos, query_seg, segment, scale)
        probs = jnp.exp(scores - log_block[:, :, None])
        grad_probs = jnp.einsum(
            "qhd,khd->hqk", grad_block, values_all, preferred_element_type=jnp.float32
        )
        inner = jnp.sum(probs * grad_probs, axis=-1, keepdims=True)
        grad_scores = (probs * (grad_probs - inner)).astype(jnp.bfloat16)
        grad_query = (
            jnp.einsum("hqk,khd->qhd", grad_scores, keys_all, preferred_element_type=jnp.float32)
            * scale
        )
        grad_keys = (
            grad_keys
            + jnp.einsum(
                "hqk,qhd->khd", grad_scores, query_block, preferred_element_type=jnp.float32
            )
            * scale
        )
        grad_values = grad_values + jnp.einsum(
            "hqk,qhd->khd",
            probs.astype(jnp.bfloat16),
            grad_block,
            preferred_element_type=jnp.float32,
        )
        return ((grad_keys, grad_values), grad_query)

    zeros_kv = jnp.zeros((length, head_count, head_dim), jnp.float32)
    blocks = (
        queries.reshape(count_blocks, block, head_count, head_dim),
        positions.reshape(count_blocks, block),
        segment.reshape(count_blocks, block),
        grad_mixed.reshape(count_blocks, block, head_count, head_dim),
        log_totals,
    )
    (grad_keys, grad_values), grad_queries = lax.scan(one_block, (zeros_kv, zeros_kv), blocks)
    return (grad_queries.reshape(length, head_count, head_dim), grad_keys, grad_values)


def local(
    tokens,
    segment_ids,
    expert_ids,
    slot_order,
    gain_attn,
    qkv_weight,
    out_weight,
    gain_ffn,
    router_weight,
    gate_up,
    down_weight,
    shared_gate_up,
    shared_down,
    cotangent,
):
    g_one, w_qkv, w_out, g_two, w_router, w_gate_up, w_down, s_gate_up, s_down = (
        lax.all_gather(gain_attn, "dp", axis=0, tiled=True),
        lax.all_gather(qkv_weight, "dp", axis=0, tiled=True),
        lax.all_gather(out_weight, "dp", axis=1, tiled=True),
        lax.all_gather(gain_ffn, "dp", axis=0, tiled=True),
        lax.all_gather(router_weight, "dp", axis=0, tiled=True),
        lax.all_gather(gate_up, "dp", axis=1, tiled=True),
        lax.all_gather(down_weight, "dp", axis=2, tiled=True),
        lax.all_gather(shared_gate_up, "dp", axis=0, tiled=True),
        lax.all_gather(shared_down, "dp", axis=1, tiled=True),
    )
    length = tokens.shape[0]
    width = tokens.shape[1]
    experts_count = w_router.shape[1]
    top_count = expert_ids.shape[1]
    capacity = length * top_count // experts_count
    head_dim = HD
    local_heads = w_qkv.shape[2] // head_dim
    scale = head_dim ** (-0.5)
    segment = segment_ids[0]
    slot_token, slot_index, kept_pair = route_slots(
        expert_ids, slot_order[0], capacity, experts_count
    )
    kept_float = kept_pair.astype(jnp.float32)
    slot_valid = slot_token < length
    slot_rows = jnp.minimum(slot_token, length - 1)
    pair_slots = jnp.minimum(slot_index, experts_count * capacity - 1)
    xfull = tokens.astype(jnp.float32)
    rms_one = rms_scale(xfull)
    xn_one = (xfull * rms_one * g_one.astype(jnp.float32)).astype(jnp.bfloat16)
    projected = jnp.einsum("td,dch->tch", xn_one, w_qkv, preferred_element_type=jnp.float32)
    cosine, sine = rotary(length, head_dim)
    queries = rotate(projected[:, 0].reshape(length, local_heads, head_dim), cosine, sine).astype(
        jnp.bfloat16
    )
    keys_all = rotate(projected[:, 1].reshape(length, local_heads, head_dim), cosine, sine).astype(
        jnp.bfloat16
    )
    values_all = projected[:, 2].reshape(length, local_heads, head_dim).astype(jnp.bfloat16)
    mixed, log_totals = attend_forward(queries, keys_all, values_all, segment, scale)
    attn_share = lax.psum_scatter(
        jnp.dot(mixed, w_out, preferred_element_type=jnp.float32),
        "tensor",
        scatter_dimension=1,
        tiled=True,
    )
    attn = lax.all_gather(attn_share, "tensor", axis=1, tiled=True)
    hidden_state = xfull + attn
    rms_two = rms_scale(hidden_state)
    xn_two = (hidden_state * rms_two * g_two.astype(jnp.float32)).astype(jnp.bfloat16)
    logits = jnp.dot(xn_two, w_router, preferred_element_type=jnp.float32)
    probs = jax.nn.softmax(logits, axis=-1)
    gates = jnp.take_along_axis(probs, expert_ids, axis=1) * kept_float
    dispatched = (xn_two[slot_rows] * slot_valid[:, None].astype(jnp.bfloat16)).reshape(
        experts_count, capacity, width
    )
    both_parts = jnp.einsum(
        "ecd,edjf->ecjf", dispatched, w_gate_up, preferred_element_type=jnp.float32
    )
    expert_hidden = silu_forward(both_parts)
    expert_out = jnp.einsum(
        "ecf,efd->ecd", expert_hidden, w_down, preferred_element_type=jnp.float32
    ).reshape(experts_count * capacity, width)
    picked = expert_out[pair_slots]
    moe = jnp.sum(gates[:, :, None] * picked, axis=1)
    shared_both = jnp.einsum("td,djf->tjf", xn_two, s_gate_up, preferred_element_type=jnp.float32)
    shared_hidden = silu_forward(shared_both)
    shared_out = jnp.dot(shared_hidden, s_down, preferred_element_type=jnp.float32)
    ffn_share = lax.psum_scatter(
        (moe + shared_out).astype(jnp.bfloat16), "tensor", scatter_dimension=1, tiled=True
    ).astype(jnp.float32)
    ffn = lax.all_gather(ffn_share.astype(jnp.bfloat16), "tensor", axis=1, tiled=True).astype(
        ffn_share.dtype
    )
    output = (hidden_state + ffn).astype(jnp.bfloat16)
    g_one, w_qkv, w_out, g_two, w_router, w_gate_up, w_down, s_gate_up, s_down = (
        lax.all_gather(gain_attn, "dp", axis=0, tiled=True),
        lax.all_gather(qkv_weight, "dp", axis=0, tiled=True),
        lax.all_gather(out_weight, "dp", axis=1, tiled=True),
        lax.all_gather(gain_ffn, "dp", axis=0, tiled=True),
        lax.all_gather(router_weight, "dp", axis=0, tiled=True),
        lax.all_gather(gate_up, "dp", axis=1, tiled=True),
        lax.all_gather(down_weight, "dp", axis=2, tiled=True),
        lax.all_gather(shared_gate_up, "dp", axis=0, tiled=True),
        lax.all_gather(shared_down, "dp", axis=1, tiled=True),
    )
    grad_y = cotangent.astype(jnp.float32)
    grad_shared_hidden = jnp.einsum(
        "td,fd->tf", cotangent, s_down, preferred_element_type=jnp.float32
    )
    grad_s_down = jnp.einsum(
        "tf,td->fd", shared_hidden, cotangent, preferred_element_type=jnp.float32
    )
    grad_shared_both = silu_back(shared_both, grad_shared_hidden)
    grad_s_gate_up = jnp.einsum(
        "td,tjf->djf", xn_two, grad_shared_both, preferred_element_type=jnp.float32
    )
    grad_xn_shared = jnp.einsum(
        "tjf,djf->td", grad_shared_both, s_gate_up, preferred_element_type=jnp.float32
    )
    slot_gate = (
        jnp.zeros((experts_count * capacity,), jnp.float32)
        .at[slot_index.reshape(-1)]
        .set(gates.reshape(-1), mode="drop")
    )
    grad_expert_out = (
        (slot_gate[:, None] * grad_y[slot_rows])
        .astype(jnp.bfloat16)
        .reshape(experts_count, capacity, width)
    )
    grad_gates_part = kept_float * jnp.sum(grad_y[:, None, :] * picked, axis=-1)
    grad_expert_hidden = jnp.einsum(
        "ecd,efd->ecf", grad_expert_out, w_down, preferred_element_type=jnp.float32
    )
    grad_w_down = jnp.einsum(
        "ecf,ecd->efd", expert_hidden, grad_expert_out, preferred_element_type=jnp.float32
    )
    grad_both = silu_back(both_parts, grad_expert_hidden)
    grad_w_gate_up = jnp.einsum(
        "ecd,ecjf->edjf", dispatched, grad_both, preferred_element_type=jnp.float32
    )
    grad_dispatched = jnp.einsum(
        "ecjf,edjf->ecd", grad_both, w_gate_up, preferred_element_type=jnp.float32
    ).reshape(experts_count * capacity, width)
    grad_xn_moe = jnp.sum(kept_float[:, :, None] * grad_dispatched[pair_slots], axis=1)
    grad_xn_part, grad_gates_share = (
        lax.psum_scatter(grad_xn_shared + grad_xn_moe, "tensor", scatter_dimension=1, tiled=True),
        lax.psum_scatter(grad_gates_part, "tensor", scatter_dimension=1, tiled=True),
    )
    grad_xn_sum, grad_gates = (
        lax.all_gather(grad_xn_part, "tensor", axis=1, tiled=True),
        lax.all_gather(grad_gates_share, "tensor", axis=1, tiled=True),
    )
    expert_match = (
        expert_ids[:, :, None] == jnp.arange(experts_count, dtype=jnp.int32)[None, None, :]
    ).astype(jnp.float32)
    grad_probs = jnp.sum(expert_match * grad_gates[:, :, None], axis=1)
    grad_logits = (
        probs * (grad_probs - jnp.sum(probs * grad_probs, axis=-1, keepdims=True))
    ).astype(jnp.bfloat16)
    grad_w_router = jnp.einsum("td,te->de", xn_two, grad_logits, preferred_element_type=jnp.float32)
    grad_xn_two = grad_xn_sum + jnp.einsum(
        "te,de->td", grad_logits, w_router, preferred_element_type=jnp.float32
    )
    grad_norm_two, grad_g_two = norm_back(
        grad_xn_two, hidden_state, rms_two, g_two.astype(jnp.float32)
    )
    grad_hidden = grad_y + grad_norm_two
    grad_attn = grad_hidden.astype(jnp.bfloat16)
    grad_w_out = jnp.einsum("th,td->hd", mixed, grad_attn, preferred_element_type=jnp.float32)
    grad_mixed = jnp.einsum(
        "td,hd->th", grad_attn, w_out, preferred_element_type=jnp.float32
    ).astype(jnp.bfloat16)
    grad_queries, grad_keys, grad_values = attend_backward(
        queries, keys_all, values_all, segment, scale, grad_mixed, log_totals
    )
    grad_projected = (
        jnp.stack(
            [rotate(grad_queries, cosine, -sine), rotate(grad_keys, cosine, -sine), grad_values],
            axis=1,
        )
        .astype(jnp.bfloat16)
        .reshape(length, 3, local_heads * head_dim)
    )
    grad_w_qkv = jnp.einsum(
        "td,tch->dch", xn_one, grad_projected, preferred_element_type=jnp.float32
    )
    grad_xn_share = lax.psum_scatter(
        jnp.einsum("tch,dch->td", grad_projected, w_qkv, preferred_element_type=jnp.float32).astype(
            jnp.bfloat16
        ),
        "tensor",
        scatter_dimension=1,
        tiled=True,
    ).astype(jnp.float32)
    grad_xn_one = lax.all_gather(
        grad_xn_share.astype(jnp.bfloat16), "tensor", axis=1, tiled=True
    ).astype(grad_xn_share.dtype)
    grad_norm_one, grad_g_one = norm_back(grad_xn_one, xfull, rms_one, g_one.astype(jnp.float32))
    grad_tokens = grad_hidden + grad_norm_one
    (
        grad_g_one,
        grad_w_qkv,
        grad_w_out,
        grad_g_two,
        grad_w_router,
        grad_w_gate_up,
        grad_w_down,
        grad_s_gate_up,
        grad_s_down,
    ) = (
        lax.psum_scatter(grad_g_one, "dp", scatter_dimension=0, tiled=True),
        lax.psum_scatter(grad_w_qkv, "dp", scatter_dimension=0, tiled=True),
        lax.psum_scatter(grad_w_out, "dp", scatter_dimension=1, tiled=True),
        lax.psum_scatter(grad_g_two, "dp", scatter_dimension=0, tiled=True),
        lax.psum_scatter(grad_w_router, "dp", scatter_dimension=0, tiled=True),
        lax.psum_scatter(grad_w_gate_up, "dp", scatter_dimension=1, tiled=True),
        lax.psum_scatter(grad_w_down, "dp", scatter_dimension=2, tiled=True),
        lax.psum_scatter(grad_s_gate_up, "dp", scatter_dimension=0, tiled=True),
        lax.psum_scatter(grad_s_down, "dp", scatter_dimension=1, tiled=True),
    )
    return (
        output,
        grad_tokens,
        grad_g_one,
        grad_w_qkv,
        grad_w_out,
        grad_g_two,
        grad_w_router,
        grad_w_gate_up,
        grad_w_down,
        grad_s_gate_up,
        grad_s_down,
    )


def solution(mesh):
    return jax.shard_map(
        local,
        mesh=mesh,
        in_specs=(
            P("dp", None),
            P("dp", None),
            P("dp", None),
            P("dp", None),
            P("dp"),
            P("dp", None, "tensor"),
            P("tensor", "dp"),
            P("dp"),
            P("dp", None),
            P(None, "dp", None, "tensor"),
            P(None, "tensor", "dp"),
            P("dp", None, "tensor"),
            P("tensor", "dp"),
            P("dp", None),
        ),
        out_specs=(
            P("dp", None),
            P("dp", None),
            P("dp"),
            P("dp", None, "tensor"),
            P("tensor", "dp"),
            P("dp"),
            P("dp", None),
            P(None, "dp", None, "tensor"),
            P(None, "tensor", "dp"),
            P("dp", None, "tensor"),
            P("tensor", "dp"),
        ),
        check_vma=False,
    )
```

profile of v0, /device:TPU:8, one launch (start us, length us, event | category | flops | bytes accessed | tf_op | source)
XLA Modules:
  0.0 1893.8 jit_solution(14494072111514062164)
XLA Ops:
  11.6 35.7 %all-reduce.6 = (bf16[768]{0:T(1024)(128)(2,1)S(1)}, bf16[768]{0:T(1024)(128)(2,1)S(1)}) all-reduce(bf16[768]{0:T(1024)(128)(2,1)S(1)} %dynamic-update-slice, bf16[768]{0:T(1024)(128)(2,1)S(1)} %dynamic-update-slice.1), channel_id=1, replica_groups=mesh['dp'=16,'tensor'=2] {'dp'}, use_global_device_ids=true, to_apply=%add | all-reduce | flops 1536 | bytes 6144
  47.4 1.4 fusion.15
  51.2 40.4 %all_gather.53 = bf16[384,768]{0,1:T(8,128)(2,1)S(1)} all-gather(bf16[384,48]{0,1:T(8,128)(2,1)} %param.20), channel_id=1, replica_groups=mesh['dp'=16,'tensor'=2] {'dp'}, dimensions={1}, use_global_device_ids=true | all-gather | bytes 626688 | tf_op jit(solution)/shard_map/all_gather | solution.py:186
  91.6 3.1 fusion.47
  97.5 1.8 copy-done.4
  101.2 1.8 fusion.80
  103.1 13.6 reduce-scatter.19.cloned.1.call-done
  120.4 4.3 scatter_custom_fusion
  126.4 4.5 gather_fusion
  131.7 4.3 scatter_custom_fusion.1
  136.2 5.3 gather_fusion.3
  141.5 3.7 copy.180
  145.2 34.5 %all-gather = bf16[16,48,4]{1,2,0:T(4,128)(2,1)S(1)} all-gather(bf16[1,48,4]{1,2,0:T(4,128)(2,1)S(1)} %bitcast.203), channel_id=1, replica_groups=mesh['dp'=16,'tensor'=2] {'dp'}, dimensions={0}, use_global_device_ids=true | all-gather | bytes 6528 | tf_op jit(solution)/shard_map/all_gather | solution.py:188
  180.7 1.7 multiply_reduce_fusion.6
  183.8 5.2 gather_fusion.1
  189.0 2.6 copy.171
  192.6 9.1 gather_fusion.5
  202.3 4.3 scatter_custom_fusion.2
  206.7 5.7 fusion.39
  212.4 48.0 %all-gather.20.cloned.1.call-done = bf16[1024,768]{0,1:T(8,128)(2,1)} async-done(((bf16[1024,48]{0,1:T(8,128)(2,1)}), bf16[1024,768]{0,1:T(8,128)(2,1)}) %all-gather.20.cloned.1.call-update) | async-done | bytes 1572880 | tf_op jit(solution)/shard_map/all_gather | solution.py:192
  260.3 6.1 fusion.36
  266.4 147.3 %all-gather.14.cloned.1.call-done = bf16[4,768,2,1024]{3,1,2,0:T(8,128)(2,1)} async-done(((bf16[4,48,2,1024]{3,1,2,0:T(8,128)(2,1)}), bf16[4,768,2,1024]{3,1,2,0:T(8,128)(2,1)}) %all-gather.14.cloned.1.call-update) | async-done | bytes 12582928 | tf_op jit(solution)/shard_map/all_gather | solution.py:189
  413.7 11.7 fusion.23
  425.5 84.9 %all-gather.16.cloned.1.call-done = bf16[4,1024,768]{1,2,0:T(8,128)(2,1)} async-done(((bf16[4,1024,48]{1,2,0:T(8,128)(2,1)}), bf16[4,1024,768]{1,2,0:T(8,128)(2,1)}) %all-gather.16.cloned.1.call-update) | async-done | bytes 6291472 | tf_op jit(solution)/shard_map/all_gather | solution.py:190
  510.4 10.6 fusion.11
  521.0 7.7 fusion
  528.7 5.3 gather_fusion.4
  533.9 3.7 reshape.406
  537.7 14.9 multiply_reduce_fusion.2
  552.6 4.2 bitcast_add_fusion
  557.2 5.3 fusion.81
  562.5 5.3 gather_fusion.2
  567.8 5.2 reshape.390
  573.0 17.0 multiply_reduce_fusion.1
  592.9 5.7 fusion.27
  600.2 4.1 all-reduce.2
  605.2 2.0 all-gather.1
  609.8 2.8 all_gather.61
  612.8 2.9 multiply_reduce_fusion.4
  615.7 1.4 subtract_add_fusion
  618.8 1.3 multiply_reduce_fusion
  620.2 1.9 multiply_convert_fusion
  623.1 1.9 fusion.28
  626.0 1.4 subtract_convert_fusion.1
  629.1 2.7 bitcast_convert_fusion
  633.5 14.4 fusion.4
  649.2 2.8 fusion.83
  653.4 1.7 fusion.49
  655.2 4.2 fusion.45
  660.1 9.0 fusion.43
  669.8 95.0 %reduce-scatter.31.cloned.1.call-done = f32[48,2,1024]{2,0,1:T(8,128)} async-done(((f32[768,2,1024]{2,0,1:T(8,128)}), f32[48,2,1024]{2,0,1:T(8,128)}) %reduce-scatter.31.cloned.1.call-update) | async-done | bytes 393232 | tf_op jit(solution)/shard_map/reduce_scatter | solution.py:381
  764.8 2.0 copy.194
  766.8 124.1 %reduce-scatter.39.cloned.1.call-done = f32[48,4]{1,0:T(8,128)} async-done(((f32[768,4]{1,0:T(8,128)}), f32[48,4]{1,0:T(8,128)}) %reduce-scatter.39.cloned.1.call-update) | async-done | bytes 784
  891.0 1.4 copy.212
  892.3 9.1 reduce-scatter.37.cloned.1.call-done
  902.7 2.4 all_gather.64
  905.8 36.7 %all-reduce.5 = (f32[768]{0:T(1024)S(1)}, f32[768]{0:T(1024)S(1)}) all-reduce(f32[768]{0:T(1024)S(1)} %get-tuple-element.138, f32[768]{0:T(1024)S(1)} %copy-done.65), channel_id=7, replica_groups=mesh['dp'=16,'tensor'=2] {'dp'}, use_global_device_ids=true, to_apply=%region_26.27.clone | all-reduce | flops 1536 | bytes 12288
  943.7 1.6 fusion.14
  945.3 326.1 %reduce-scatter.27.cloned.1.call-done = f32[4,48,2,1024]{3,1,2,0:T(8,128)} async-done(((f32[4,768,2,1024]{3,1,2,0:T(8,128)}), f32[4,48,2,1024]{3,1,2,0:T(8,128)}) %reduce-scatter.27.cloned.1.call-update) | async-done | bytes 1572880 | tf_op jit(solution)/shard_map/reduce_scatter | solution.py:379
  1271.4 3.8 copy.193
  1275.2 133.5 %reduce-scatter.33.cloned.1.call-done = f32[1024,48]{0,1:T(8,128)} async-done(((f32[1024,768]{0,1:T(8,128)}), f32[1024,48]{0,1:T(8,128)}) %reduce-scatter.33.cloned.1.call-update) | async-done | bytes 196624 | tf_op jit(solution)/shard_map/reduce_scatter | solution.py:382
  1408.7 128.4 %reduce-scatter.25.cloned.1.call-done = f32[384,48]{0,1:T(8,128)} async-done(((f32[384,768]{0,1:T(8,128)}), f32[384,48]{0,1:T(8,128)}) %reduce-scatter.25.cloned.1.call-update) | async-done | bytes 73744 | tf_op jit(solution)/shard_map/reduce_scatter | solution.py:376
  1537.1 139.2 %reduce-scatter.23.cloned.1.call-done = f32[48,3,384]{2,0,1:T(8,128)} async-done(((f32[768,3,384]{2,0,1:T(8,128)}), f32[48,3,384]{2,0,1:T(8,128)}) %reduce-scatter.23.cloned.1.call-update) | async-done | bytes 221200 | tf_op jit(solution)/shard_map/reduce_scatter | solution.py:375
  1676.3 210.2 %reduce-scatter.29.cloned.1.call-done = f32[4,1024,48]{1,2,0:T(8,128)} async-done(((f32[4,1024,768]{1,2,0:T(8,128)}), f32[4,1024,48]{1,2,0:T(8,128)}) %reduce-scatter.29.cloned.1.call-update) | async-done | bytes 786448 | tf_op jit(solution)/shard_map/reduce_scatter | solution.py:380
  (288 shorter events, 42.7 us)
Async XLA Ops:
  7.2 84.4 %all-gather.10.cloned.1.call-start = ((), (), s32[]{:S(2)}) async-start(), calls=%async_computation.11 | async-start | bytes 1880064 | tf_op jit(solution)/shard_map/all_gather | solution.py:185
  7.9 108.7 %reduce-scatter.19.cloned.1.call-start = ((), (), s32[]{:S(2)}) async-start(), calls=%async_computation.12 | async-start | bytes 2359296 | tf_op jit(solution)/shard_map/reduce_scatter | solution.py:223
  47.3 47.4 %copy-start.59 = (f32[768]{0:T(1024)}, f32[768]{0:T(1024)S(1)}, u32[]{:S(2)}) copy-start(f32[768]{0:T(1024)S(1)} %convert_element_type.177) | copy-start | bytes 9220
  49.3 45.4 %copy-start.63 = (f32[512]{0:T(512)}, f32[512]{0:T(512)S(1)}, u32[]{:S(2)}) copy-start(f32[512]{0:T(512)S(1)} %get-tuple-element.176) | copy-start | bytes 6148
  50.3 44.7 %copy-start.32 = (f32[512,32]{0,1:T(8,128)}, f32[512,32]{0,1:T(8,128)S(1)}, u32[]{:S(2)}) copy-start(f32[512,32]{0,1:T(8,128)S(1)} %get-tuple-element.174) | copy-start | bytes 196612
  91.6 8.9 copy-start.15
  96.6 2.7 copy-start.4
  96.6 2.7 copy-start.51
  97.4 3.0 copy-start.53
  101.2 15.5 copy-start.41
  103.0 15.1 copy-start.31
  103.0 77.6 %all-gather.12.cloned.1.call-start = ((), (), s32[]{:S(2)}) async-start(), calls=%async_computation.13 | async-start | bytes 2359296 | tf_op jit(solution)/shard_map/all_gather | solution.py:229
  116.6 3.4 copy-start.44
  116.7 3.7 copy-start.68
  116.7 90.0 %all-gather.18.cloned.1.call-start = ((), (), s32[]{:S(2)}) async-start(), calls=%async_computation.16 | async-start | bytes 3342336 | tf_op jit(solution)/shard_map/all_gather | solution.py:191
  117.5 142.9 %all-gather.20.cloned.1.call-start = ((), (), s32[]{:S(2)}) async-start(), calls=%async_computation.17 | async-start | bytes 1671168 | tf_op jit(solution)/shard_map/all_gather | solution.py:192
  118.0 295.7 %all-gather.14.cloned.1.call-start = ((), (), s32[]{:S(2)}) async-start(), calls=%async_computation.14 | async-start | bytes 13369344 | tf_op jit(solution)/shard_map/all_gather | solution.py:189
  119.2 391.1 %all-gather.16.cloned.1.call-start = ((), (), s32[]{:S(2)}) async-start(), calls=%async_computation.15 | async-start | bytes 6684672 | tf_op jit(solution)/shard_map/all_gather | solution.py:190
  120.0 472.4 %reduce-scatter.21.cloned.1.call-start = ((), (), s32[]{:S(2)}) async-start(), calls=%async_computation.18 | async-start | bytes 2359296 | tf_op jit(solution)/shard_map/reduce_scatter | solution.py:309
  120.0 63.0 %copy-start.49 = (f32[768]{0:T(1024)}, f32[768]{0:T(1024)S(1)}, u32[]{:S(2)}) copy-start(f32[768]{0:T(1024)S(1)} %convert_element_type.186) | copy-start | bytes 9220
  126.4 9.6 copy-start.13
  136.0 277.7 %copy-start.42 = (bf16[4,256]{1,0:T(4,128)(2,1)}, bf16[4,256]{1,0:T(4,128)(2,1)S(1)}, u32[]{:S(2)}) copy-start(bf16[4,256]{1,0:T(4,128)(2,1)S(1)} %reshape.372) | copy-start | bytes 6148
  136.1 5.3 copy-start
  141.5 3.7 copy-start.69
  141.5 39.2 %copy-start.11 = (bf16[512,768]{1,0:T(8,128)(2,1)S(1)}, bf16[512,768]{1,0:T(8,128)(2,1)}, u32[]{:S(2)}) copy-start(bf16[512,768]{1,0:T(8,128)(2,1)} %param.14) | copy-start | bytes 2359300
  179.8 11.8 copy-start.55
  182.4 6.6 copy-start.5
  183.8 22.9 %copy-start.2 = (bf16[512,768]{1,0:T(8,128)(2,1)}, bf16[512,768]{1,0:T(8,128)(2,1)S(1)}, u32[]{:S(2)}) copy-start(bf16[512,768]{1,0:T(8,128)(2,1)S(1)} %multiply_convert_fusion.8) | copy-start | bytes 2359300
  192.5 9.1 copy-start.57
  206.6 303.7 %copy-start.45 = (f32[4,256]{1,0:T(4,128)}, f32[4,256]{1,0:T(4,128)S(1)}, u32[]{:S(2)}) copy-start(f32[4,256]{1,0:T(4,128)S(1)} %mul.612) | copy-start | bytes 12292
  266.4 244.0 %copy-start.9 = (f32[4,256,768]{1,2,0:T(8,128)S(1)}, f32[4,256,768]{1,2,0:T(8,128)}, u32[]{:S(2)}) copy-start(f32[4,256,768]{1,2,0:T(8,128)} %copy.180) | copy-start | bytes 9437188
  537.7 14.9 copy-start.70
  537.7 14.9 copy-start.73
  556.9 51.7 %reduce-scatter.35.cloned.1.call-start = ((), (), s32[]{:S(2)}) async-start(), calls=%async_computation.26 | async-start | bytes 1179648
  567.8 5.2 copy-start.1
  573.0 17.0 copy-start.17
  573.0 17.0 copy-start.71
  592.3 20.5 %all-gather.22.cloned.1.call-start = ((), (), s32[]{:S(2)}) async-start(), calls=%async_computation.19 | async-start | bytes 2359296 | tf_op jit(solution)/shard_map/all_gather | solution.py:313
  592.9 171.9 %reduce-scatter.31.cloned.1.call-start = ((), (), s32[]{:S(2)}) async-start(), calls=%async_computation.24 | async-start | bytes 6684672 | tf_op jit(solution)/shard_map/reduce_scatter | solution.py:381
  598.6 8.7 copy-start.39
  598.6 8.7 copy-start.48
  598.6 8.7 copy-start.58
  598.7 292.3 %reduce-scatter.39.cloned.1.call-start = ((), (), s32[]{:S(2)}) async-start(), calls=%async_computation.28 | async-start | bytes 417792
  600.1 12.6 copy-start.6
  600.2 12.6 copy-start.50
  600.2 12.6 copy-start.56
  600.2 12.6 copy-start.62
  608.5 293.0 %reduce-scatter.37.cloned.1.call-start = ((), (), s32[]{:S(2)}) async-start(), calls=%async_computation.27 | async-start | bytes 1179648
  612.7 3.0 copy-start.14
  612.7 3.0 copy-start.67
  612.8 4.9 slice-start
  623.1 2.9 copy-start.33
  623.1 2.9 copy-start.40
  633.0 638.4 %reduce-scatter.27.cloned.1.call-start = ((), (), s32[]{:S(2)}) async-start(), calls=%async_computation.22 | async-start | bytes 26738688 | tf_op jit(solution)/shard_map/reduce_scatter | solution.py:379
  647.9 760.7 %reduce-scatter.33.cloned.1.call-start = ((), (), s32[]{:S(2)}) async-start(), calls=%async_computation.25 | async-start | bytes 3342336 | tf_op jit(solution)/shard_map/reduce_scatter | solution.py:382
  651.9 3.2 copy-start.12
  652.0 3.2 copy-start.36
  652.0 3.2 copy-start.60
  652.0 3.2 copy-start.64
  652.0 885.1 %reduce-scatter.25.cloned.1.call-start = ((), (), s32[]{:S(2)}) async-start(), calls=%async_computation.21 | async-start | bytes 1253376 | tf_op jit(solution)/shard_map/reduce_scatter | solution.py:376
  655.1 1021.2 %reduce-scatter.23.cloned.1.call-start = ((), (), s32[]{:S(2)}) async-start(), calls=%async_computation.20 | async-start | bytes 3760128 | tf_op jit(solution)/shard_map/reduce_scatter | solution.py:375
  659.5 1227.1 %reduce-scatter.29.cloned.1.call-start = ((), (), s32[]{:S(2)}) async-start(), calls=%async_computation.23 | async-start | bytes 13369344 | tf_op jit(solution)/shard_map/reduce_scatter | solution.py:380
  669.8 236.0 %copy-start.65 = (f32[768]{0:T(1024)S(1)}, f32[768]{0:T(1024)}, u32[]{:S(2)}) copy-start(f32[768]{0:T(1024)} %get-tuple-element.134) | copy-start | bytes 9220
  669.8 273.9 %copy-start.66 = (f32[512]{0:T(512)S(1)}, f32[512]{0:T(512)}, u32[]{:S(2)}) copy-start(f32[512]{0:T(512)} %get-tuple-element.175) | copy-start | bytes 6148
  (31 other events, 40.6 us)
Sparse Core Ops, SparseCore 0:
  10.7 62.5 all-gather.9
  103.1 13.4 reduce-scatter.18
  118.2 10.9 all-gather.11
  132.7 69.1 all-gather.17
  204.9 55.3 all-gather.19
  263.8 149.8 all-gather.13
  416.7 93.5 all-gather.15
  557.0 8.2 reduce-scatter.20
  592.4 7.3 reduce-scatter.34
  601.3 11.4 all-gather.21
  618.9 145.8 reduce-scatter.30
  770.0 120.9 reduce-scatter.38
  893.8 7.6 reduce-scatter.36
  908.0 363.3 reduce-scatter.26
  1277.6 131.0 reduce-scatter.32
  1414.6 122.5 reduce-scatter.24
  1543.4 132.8 reduce-scatter.22
  1683.3 203.1 reduce-scatter.28
where the time goes:
time: 1900 us; the launch traced here: 1890 us
  waiting for transfers between devices  1460 us (77%)
  blocking collectives  159 us (8%)
  matrix products  110 us (6%)
  local copies, waits for them, and re-layouts  96.4 us (5%)
  other arithmetic  48.2 us (3%)
    reduce_scatter x1, waiting for transfers between devices, local(): lax.psum_scatter(grad_w_gate_up, 'dp', scatter_dimension=1, tiled=True)  326 us
    reduce_scatter x1, waiting for transfers between devices, local(): lax.psum_scatter(grad_w_down, 'dp', scatter_dimension=2, tiled=True)  210 us
    all_gather x1, waiting for transfers between devices, local(): lax.all_gather(gate_up, 'dp', axis=1, tiled=True)  147 us
    reduce_scatter x1, waiting for transfers between devices, local(): lax.psum_scatter(grad_w_qkv, 'dp', scatter_dimension=0, tiled=True)  139 us
    unnamed x21, waiting for transfers between devices  136 us
    reduce_scatter x1, waiting for transfers between devices, local(): lax.psum_scatter(grad_s_down, 'dp', scatter_dimension=1, tiled=True)  133 us
    reduce_scatter x1, waiting for transfers between devices, local(): lax.psum_scatter(grad_w_out, 'dp', scatter_dimension=1, tiled=True)  128 us
    reduce_scatter x1, waiting for transfers between devices, local(): lax.psum_scatter(grad_s_gate_up, 'dp', scatter_dimension=0, tiled=True)  95 us
  transfers between devices with their start and end apart: 18, of which 13 were waited for; matrix products, arithmetic and copies ran while one was open for 10% of the time, Pallas kernels for 0%

commit v1 on v0

--- a/solution.py
+++ b/solution.py
@@ -1,11 +1,16 @@
+import functools
 import math
 
 import jax
 import jax.numpy as jnp
 from jax import lax
+from jax.experimental import pallas as pl
+from jax.experimental.pallas import tpu as pltpu
 from jax.sharding import PartitionSpec as P
 
 HD = 64
+GROUP = 4
+MESH = pl.DeviceIdType.MESH
 
 
 epsilon = 1e-06
@@ -164,7 +169,14 @@
     return (grad_queries.reshape(length, head_count, head_dim), grad_keys, grad_values)
 
 
-def local(
+def sum_rows(grad, axis, scatter_dimension, tiled):
+    part = lax.psum_scatter(
+        grad.astype(jnp.bfloat16), axis, scatter_dimension=scatter_dimension, tiled=tiled
+    )
+    return part.astype(jnp.float32)
+
+
+def local_plain(
     tokens,
     segment_ids,
     expert_ids,
@@ -255,17 +267,6 @@
         ffn_share.dtype
     )
     output = (hidden_state + ffn).astype(jnp.bfloat16)
-    g_one, w_qkv, w_out, g_two, w_router, w_gate_up, w_down, s_gate_up, s_down = (
-        lax.all_gather(gain_attn, "dp", axis=0, tiled=True),
-        lax.all_gather(qkv_weight, "dp", axis=0, tiled=True),
-        lax.all_gather(out_weight, "dp", axis=1, tiled=True),
-        lax.all_gather(gain_ffn, "dp", axis=0, tiled=True),
-        lax.all_gather(router_weight, "dp", axis=0, tiled=True),
-        lax.all_gather(gate_up, "dp", axis=1, tiled=True),
-        lax.all_gather(down_weight, "dp", axis=2, tiled=True),
-        lax.all_gather(shared_gate_up, "dp", axis=0, tiled=True),
-        lax.all_gather(shared_down, "dp", axis=1, tiled=True),
-    )
     grad_y = cotangent.astype(jnp.float32)
     grad_shared_hidden = jnp.einsum(
         "td,fd->tf", cotangent, s_down, preferred_element_type=jnp.float32
@@ -372,14 +373,14 @@
         grad_s_down,
     ) = (
         lax.psum_scatter(grad_g_one, "dp", scatter_dimension=0, tiled=True),
-        lax.psum_scatter(grad_w_qkv, "dp", scatter_dimension=0, tiled=True),
-        lax.psum_scatter(grad_w_out, "dp", scatter_dimension=1, tiled=True),
+        sum_rows(grad_w_qkv, "dp", scatter_dimension=0, tiled=True),
+        sum_rows(grad_w_out, "dp", scatter_dimension=1, tiled=True),
         lax.psum_scatter(grad_g_two, "dp", scatter_dimension=0, tiled=True),
         lax.psum_scatter(grad_w_router, "dp", scatter_dimension=0, tiled=True),
-        lax.psum_scatter(grad_w_gate_up, "dp", scatter_dimension=1, tiled=True),
-        lax.psum_scatter(grad_w_down, "dp", scatter_dimension=2, tiled=True),
-        lax.psum_scatter(grad_s_gate_up, "dp", scatter_dimension=0, tiled=True),
-        lax.psum_scatter(grad_s_down, "dp", scatter_dimension=1, tiled=True),
+        sum_rows(grad_w_gate_up, "dp", scatter_dimension=1, tiled=True),
+        sum_rows(grad_w_down, "dp", scatter_dimension=2, tiled=True),
+        sum_rows(grad_s_gate_up, "dp", scatter_dimension=0, tiled=True),
+        sum_rows(grad_s_down, "dp", scatter_dimension=1, tiled=True),
     )
     return (
         output,
@@ -396,9 +397,636 @@
     )
 
 
+class Place:
+    def __init__(self, planes):
+        d = lax.axis_index("dp")
+        self.planes = planes
+        self.d, self.c = d, lax.axis_index("tensor")
+        self.z, self.p = d // GROUP, lax.rem(d, GROUP)
+        bit0, bit1 = lax.rem(self.p, 2), self.p // 2
+        flip0, flip1 = 1 - bit0, 1 - bit1
+        self.member = [
+            self.p,
+            flip0 + 2 * bit1,
+            bit0 + 2 * flip1,
+            flip0 + 2 * flip1,
+        ]
+
+    def near(self, j):
+        return (self.z * GROUP + self.member[j], self.c)
+
+    def up(self):
+        return (self.d + GROUP, self.c)
+
+    def down(self):
+        return (self.d - GROUP, self.c)
+
+    def when(self, condition, action):
+        pl.when(condition)(action)
+
+    def has_up(self, k=1):
+        return self.z + k < self.planes
+
+    def has_down(self, k=1):
+        return self.z - k >= 0
+
+    def greet(self):
+        barrier = pltpu.get_barrier_semaphore()
+
+        def hello(device):
+            pl.semaphore_signal(barrier, inc=1, device_id=device, device_id_type=MESH)
+
+        for j in range(1, GROUP):
+            hello(self.near(j))
+        self.when(self.has_up(), lambda: hello(self.up()))
+        self.when(self.has_down(), lambda: hello(self.down()))
+        line = self.has_up().astype(jnp.int32) + self.has_down().astype(jnp.int32)
+        pl.semaphore_wait(barrier, GROUP - 1 + line)
+
+
+def send(source, target, send_sem, recv_sem, device):
+    return pltpu.make_async_remote_copy(
+        src_ref=source,
+        dst_ref=target,
+        send_sem=send_sem,
+        recv_sem=recv_sem,
+        device_id=device,
+        device_id_type=MESH,
+    )
+
+
+def gather_kernel(planes, s_ref, e_ref, s_all, e_all, local_sem, s_recv, e_recv, s_send, e_send):
+    at = Place(planes)
+    own = at.d
+
+    def s_copy(block, source, way, device):
+        return send(source, s_all.at[block], s_send.at[way, block], s_recv.at[block], device)
+
+    def e_copy(block, source, way, device):
+        return send(source, e_all.at[block], e_send.at[way, block], e_recv.at[block], device)
+
+    def s_landed(block):
+        s_copy(block, s_ref, 0, at.near(1)).wait_recv()
+
+    def e_landed(block):
+        e_copy(block, e_ref.at[0], 0, at.near(1)).wait_recv()
+
+    at.greet()
+    keep_s = pltpu.make_async_copy(s_ref, s_all.at[own], local_sem.at[0])
+    keep_e = pltpu.make_async_copy(e_ref.at[at.p], e_all.at[own], local_sem.at[1])
+    keep_s.start()
+    keep_e.start()
+    for j in range(1, GROUP):
+        send(
+            e_ref.at[at.member[j]],
+            e_all.at[own],
+            e_send.at[1 + j, own],
+            e_recv.at[own],
+            at.near(j),
+        ).start()
+    at.when(at.has_up(), lambda: s_copy(own, s_ref, 0, at.up()).start())
+    at.when(at.has_down(), lambda: s_copy(own, s_ref, 1, at.down()).start())
+    s_copy(own, s_ref, 2, at.near(1)).start()
+    s_copy(own, s_ref, 3, at.near(2)).start()
+    at.when(at.has_up(), lambda: e_copy(own, e_ref.at[at.p], 0, at.up()).start())
+    at.when(at.has_down(), lambda: e_copy(own, e_ref.at[at.p], 1, at.down()).start())
+
+    for j in range(1, GROUP):
+        block = at.z * GROUP + at.member[j]
+        e_landed(block)
+        at.when(at.has_up(), lambda: e_copy(block, e_all.at[block], 0, at.up()).start())
+        at.when(at.has_down(), lambda: e_copy(block, e_all.at[block], 1, at.down()).start())
+
+    def cross(plane):
+        first = plane * GROUP + at.member[1]
+        second = plane * GROUP + at.member[2]
+        even = lax.rem(plane, 2) == 0
+        s_landed(first)
+        at.when(even, lambda: s_copy(first, s_all.at[first], 3, at.near(2)).start())
+        s_landed(second)
+        at.when(
+            jnp.logical_not(even),
+            lambda: s_copy(second, s_all.at[second], 2, at.near(1)).start(),
+        )
+
+    def spread(plane, onward, device_of):
+        block = plane * GROUP + at.p
+        s_landed(block)
+        at.when(onward[0], lambda: s_copy(block, s_all.at[block], onward[1], device_of()).start())
+        s_copy(block, s_all.at[block], 2, at.near(1)).start()
+        s_copy(block, s_all.at[block], 3, at.near(2)).start()
+
+    def pass_on(plane, onward, device_of):
+        for j in range(GROUP):
+            block = plane * GROUP + at.member[j]
+            e_landed(block)
+            at.when(
+                onward[0], lambda: e_copy(block, e_all.at[block], onward[1], device_of()).start()
+            )
+
+    cross(at.z)
+    for k in range(1, planes):
+        below, above = at.z - k, at.z + k
+        at.when(at.has_down(k), lambda: spread(below, (at.has_up(), 0), at.up))
+        at.when(at.has_up(k), lambda: spread(above, (at.has_down(), 1), at.down))
+        at.when(at.has_down(k), lambda: pass_on(below, (at.has_up(), 0), at.up))
+        at.when(at.has_up(k), lambda: pass_on(above, (at.has_down(), 1), at.down))
+        at.when(at.has_down(k), lambda: cross(below))
+        at.when(at.has_up(k), lambda: cross(above))
+
+    keep_s.wait()
+    keep_e.wait()
+    for j in range(1, GROUP):
+        send(
+            e_ref.at[at.member[j]],
+            e_all.at[own],
+            e_send.at[1 + j, own],
+            e_recv.at[own],
+            at.near(j),
+        ).wait_send()
+    for plane in range(planes):
+        s_landed(plane * GROUP + at.member[3])
+        block = plane * GROUP + at.p
+        s_copy(block, s_ref, 2, at.near(1)).wait_send()
+        s_copy(block, s_ref, 3, at.near(2)).wait_send()
+        if plane % 2 == 0:
+            s_copy(plane * GROUP + at.member[1], s_ref, 3, at.near(2)).wait_send()
+        else:
+            s_copy(plane * GROUP + at.member[2], s_ref, 2, at.near(1)).wait_send()
+
+        def sent(way, device_of):
+            s_copy(block, s_ref, way, device_of()).wait_send()
+            for q in range(GROUP):
+                e_copy(plane * GROUP + q, e_ref.at[0], way, device_of()).wait_send()
+
+        at.when((at.z >= plane) & at.has_up(), lambda: sent(0, at.up))
+        at.when((at.z <= plane) & at.has_down(), lambda: sent(1, at.down))
+
+
+def gather_weights(planes, shared, expert):
+    n = planes * GROUP
+    anywhere = pl.BlockSpec(memory_space=pl.ANY)
+    return pl.pallas_call(
+        functools.partial(gather_kernel, planes),
+        out_shape=(
+            jax.ShapeDtypeStruct((n,) + shared.shape, shared.dtype),
+            jax.ShapeDtypeStruct((n,) + expert.shape[1:], expert.dtype),
+        ),
+        in_specs=[anywhere, anywhere],
+        out_specs=(anywhere, anywhere),
+        scratch_shapes=[
+            pltpu.SemaphoreType.DMA((2,)),
+            pltpu.SemaphoreType.DMA((n,)),
+            pltpu.SemaphoreType.DMA((n,)),
+            pltpu.SemaphoreType.DMA((4, n)),
+            pltpu.SemaphoreType.DMA((1 + GROUP, n)),
+        ],
+        compiler_params=pltpu.CompilerParams(collective_id=0, has_side_effects=True),
+    )(shared, expert)
+
+
+def reduce_kernel(
+    planes,
+    s_ref,
+    e_ref,
+    s_out,
+    e_out,
+    s_one,
+    s_two,
+    s_below,
+    s_above,
+    e_below,
+    e_above,
+    e_last,
+    one_send,
+    one_recv,
+    two_send,
+    two_recv,
+    s_send,
+    s_recv,
+    e_send,
+    e_recv,
+    last_send,
+    last_recv,
+):
+    at = Place(planes)
+    f32 = jnp.float32
+
+    def one_copy(plane, i, even):
+        j = 1 if even else 2
+        target = at.member[3] if i else at.member[j]
+        return send(
+            s_ref.at[plane * GROUP + target],
+            s_one.at[plane, i],
+            one_send.at[plane, i],
+            one_recv.at[plane, i],
+            at.near(j),
+        )
+
+    def two_copy(plane, even):
+        j = 2 if even else 1
+        return send(
+            s_one.at[plane, 1],
+            s_two.at[plane],
+            two_send.at[plane],
+            two_recv.at[plane],
+            at.near(j),
+        )
+
+    def by_parity(plane, action):
+        even = lax.rem(plane, 2) == 0
+        at.when(even, lambda: action(True))
+        at.when(jnp.logical_not(even), lambda: action(False))
+
+    def s_line(source, plane, way):
+        target, device = (s_below, at.up()) if way == 0 else (s_above, at.down())
+        return send(source, target.at[plane], s_send.at[way, plane], s_recv.at[way, plane], device)
+
+    def e_line(source, block, way):
+        target, device = (e_below, at.up()) if way == 0 else (e_above, at.down())
+        return send(source, target.at[block], e_send.at[way, block], e_recv.at[way, block], device)
+
+    def last_copy(j):
+        return send(
+            e_ref.at[0],
+            e_last.at[j],
+            last_send.at[j],
+            last_recv.at[j],
+            at.near(j),
+        )
+
+    at.greet()
+
+    def e_step(plane, way):
+        behind = at.has_down() if way == 0 else at.has_up()
+        held = e_below if way == 0 else e_above
+        for j in range(GROUP):
+            block = plane * GROUP + at.member[j]
+
+            def add():
+                e_line(e_ref.at[block], block, way).wait_recv()
+                held[block] = (held[block].astype(f32) + e_ref[block].astype(f32)).astype(
+                    held.dtype
+                )
+                e_line(held.at[block], block, way).start()
+
+            at.when(behind, add)
+            at.when(jnp.logical_not(behind), lambda: e_line(e_ref.at[block], block, way).start())
+
+    def plane_sum(plane):
+        def stage(even):
+            mine = plane * GROUP + at.p
+            other = plane * GROUP + (at.member[2] if even else at.member[1])
+            one_copy(plane, 1, even).wait_recv()
+            s_one[plane, 1] = (s_one[plane, 1].astype(f32) + s_ref[other].astype(f32)).astype(
+                s_one.dtype
+            )
+            two_copy(plane, even).start()
+            one_copy(plane, 0, even).wait_recv()
+            two_copy(plane, even).wait_recv()
+            s_two[plane] = (
+                s_two[plane].astype(f32) + s_one[plane, 0].astype(f32) + s_ref[mine].astype(f32)
+            ).astype(s_two.dtype)
+
+        by_parity(plane, stage)
+
+    def s_step(plane, way):
+        plane_sum(plane)
+        behind = at.has_down() if way == 0 else at.has_up()
+        held = s_below if way == 0 else s_above
+
+        def add():
+            s_line(s_two.at[plane], plane, way).wait_recv()
+            held[plane] = (held[plane].astype(f32) + s_two[plane].astype(f32)).astype(held.dtype)
+            s_line(held.at[plane], plane, way).start()
+
+        at.when(behind, add)
+        at.when(jnp.logical_not(behind), lambda: s_line(s_two.at[plane], plane, way).start())
+
+    def both_ways(action, k):
+        at.when(at.has_up(k), lambda: action(at.z + k, 0))
+        at.when(at.has_down(k), lambda: action(at.z - k, 1))
+
+    def start_one(plane, way):
+        def go(even):
+            one_copy(plane, 1, even).start()
+            one_copy(plane, 0, even).start()
+
+        by_parity(plane, go)
+
+    for k in range(planes - 1, 0, -1):
+        both_ways(start_one, k)
+    start_one(at.z, 0)
+    for k in range(planes - 1, 0, -1):
+        both_ways(e_step, k)
+        both_ways(s_step, k)
+
+    for j in range(GROUP):
+        block = at.z * GROUP + at.member[j]
+        at.when(at.has_down(), lambda: e_line(e_ref.at[block], block, 0).wait_recv())
+        at.when(at.has_up(), lambda: e_line(e_ref.at[block], block, 1).wait_recv())
+        low = jnp.where(at.has_down(), e_below[block].astype(f32), 0.0)
+        high = jnp.where(at.has_up(), e_above[block].astype(f32), 0.0)
+        total = e_ref[block].astype(f32) + low + high
+        if j == 0:
+            e_out[at.p] = total
+        else:
+            e_below[block] = total.astype(e_below.dtype)
+            send(
+                e_below.at[block],
+                e_last.at[j],
+                last_send.at[j],
+                last_recv.at[j],
+                at.near(j),
+            ).start()
+    plane_sum(at.z)
+    at.when(at.has_down(), lambda: s_line(s_two.at[at.z], at.z, 0).wait_recv())
+    at.when(at.has_up(), lambda: s_line(s_two.at[at.z], at.z, 1).wait_recv())
+    low = jnp.where(at.has_down(), s_below[at.z].astype(f32), 0.0)
+    high = jnp.where(at.has_up(), s_above[at.z].astype(f32), 0.0)
+    s_out[...] = s_two[at.z].astype(f32) + low + high
+    for j in range(1, GROUP):
+        last_copy(j).wait_recv()
+        e_out[at.member[j]] = e_last[j].astype(f32)
+
+    for j in range(1, GROUP):
+        last_copy(j).wait_send()
+    for plane in range(planes):
+        even = plane % 2 == 0
+        one_copy(plane, 0, even).wait_send()
+        one_copy(plane, 1, even).wait_send()
+        two_copy(plane, even).wait_send()
+
+        def sent(way):
+            s_line(s_two.at[plane], plane, way).wait_send()
+            for q in range(GROUP):
+                block = plane * GROUP + q
+                e_line(e_ref.at[block], block, way).wait_send()
+
+        at.when(at.z < plane, lambda: sent(0))
+        at.when(at.z > plane, lambda: sent(1))
+
+
+def reduce_grads(planes, shared, expert):
+    n, rows, s_width = shared.shape
+    e_width = expert.shape[2]
+    vmem = pl.BlockSpec(memory_space=pltpu.VMEM)
+    bf16, dma = jnp.bfloat16, pltpu.SemaphoreType.DMA
+    return pl.pallas_call(
+        functools.partial(reduce_kernel, planes),
+        out_shape=(
+            jax.ShapeDtypeStruct((rows, s_width), jnp.float32),
+            jax.ShapeDtypeStruct((GROUP, rows, e_width), jnp.float32),
+        ),
+        in_specs=[vmem, vmem],
+        out_specs=(vmem, vmem),
+        scratch_shapes=[
+            pltpu.VMEM((planes, 2, rows, s_width), bf16),
+            pltpu.VMEM((planes, rows, s_width), bf16),
+            pltpu.VMEM((planes, rows, s_width), bf16),
+            pltpu.VMEM((planes, rows, s_width), bf16),
+            pltpu.VMEM((n, rows, e_width), bf16),
+            pltpu.VMEM((n, rows, e_width), bf16),
+            pltpu.VMEM((GROUP, rows, e_width), bf16),
+            dma((planes, 2)),
+            dma((planes, 2)),
+            dma((planes,)),
+            dma((planes,)),
+            dma((2, planes)),
+            dma((2, planes)),
+            dma((2, n)),
+            dma((2, n)),
+            dma((GROUP,)),
+            dma((GROUP,)),
+        ],
+        compiler_params=pltpu.CompilerParams(
+            collective_id=1, has_side_effects=True, vmem_limit_bytes=60 << 20
+        ),
+    )(shared, expert)
+
+
+def other_core(values):
+    return lax.ppermute(values, "tensor", [(0, 1), (1, 0)])
+
+
+def add_cores(values):
+    return values + other_core(values)
+
+
+def to_members(planes, blocks):
+    out = [blocks[0]]
+    for j in range(1, GROUP):
+        order = [(d, (d // GROUP) * GROUP + ((d % GROUP) ^ j)) for d in range(planes * GROUP)]
+        out.append(lax.ppermute(blocks[j], "dp", order))
+    return jnp.stack(out)
+
+
+def local_grouped(
+    planes,
+    tokens,
+    segment_ids,
+    expert_ids,
+    slot_order,
+    gain_attn,
+    qkv_weight,
+    out_weight,
+    gain_ffn,
+    router_weight,
+    gate_up,
+    down_weight,
+    shared_gate_up,
+    shared_down,
+    cotangent,
+):
+    bf16, f32 = jnp.bfloat16, jnp.float32
+    rows, heads_width = qkv_weight.shape[0], qkv_weight.shape[2]
+    experts, hidden = down_weight.shape[0], down_weight.shape[1]
+    s_hidden = shared_down.shape[0]
+    length, width = tokens.shape
+    top = expert_ids.shape[1]
+    capacity = length * top // experts
+    heads = heads_width // HD
+    scale = HD ** (-0.5)
+    n = planes * GROUP
+    cuts = [2 * s_hidden, s_hidden, 3 * heads_width, heads_width, 128]
+    edges = [sum(cuts[:i]) for i in range(len(cuts) + 1)]
+
+    def part(array, i):
+        return array[..., edges[i] : edges[i + 1]]
+
+    small = jnp.concatenate([gain_attn[:, None], gain_ffn[:, None], router_weight], axis=1)
+    small = jnp.pad(small, ((0, 0), (0, 128 - small.shape[1])))
+    packed = jnp.concatenate(
+        [
+            shared_gate_up.reshape(rows, 2 * s_hidden),
+            shared_down.T,
+            qkv_weight.reshape(rows, 3 * heads_width),
+            out_weight.T,
+            small,
+        ],
+        axis=1,
+    )
+    expert_packed = jnp.concatenate(
+        [gate_up.reshape(experts, rows, 2 * hidden), down_weight.transpose(0, 2, 1)], axis=2
+    )
+    all_packed, all_expert = gather_weights(planes, packed, expert_packed)
+    all_packed = all_packed.reshape(width, -1)
+    all_expert = all_expert.reshape(width, -1)
+    s_gate_up, s_down_t, w_qkv, w_out_t = (part(all_packed, i) for i in range(4))
+    small_all = part(all_packed, 4)
+    g_one, g_two = small_all[:, 0].astype(f32), small_all[:, 1].astype(f32)
+    w_router = small_all[:, 2 : 2 + experts]
+    w_gate_up, w_down_t = all_expert[:, : 2 * hidden], all_expert[:, 2 * hidden :]
+
+    def mm(spec, a, b):
+        return jnp.einsum(spec, a, b, preferred_element_type=f32)
+
+    member = lax.rem(lax.axis_index("dp"), GROUP)
+    pair_expert = expert_ids.reshape(-1)
+    order = slot_order[0]
+    ahead = (pair_expert[None, :] == pair_expert[:, None]) & (order[None, :] < order[:, None])
+    position = jnp.sum(ahead.astype(jnp.int32), axis=1)
+    kept = (position < capacity).reshape(length, top)
+    slot = jnp.where(
+        kept, (jnp.bitwise_xor(pair_expert, member) * capacity + position).reshape(length, top), -1
+    )
+    kept_float = kept.astype(f32)
+    slots = jnp.arange(experts * capacity, dtype=jnp.int32)
+    pick = [(slot[:, r : r + 1] == slots[None, :]).astype(bf16) for r in range(top)]
+    pick_any = sum(pick[1:], pick[0])
+
+    segment = segment_ids[0]
+    xfull = tokens.astype(f32)
+    rms_one = rms_scale(xfull)
+    xn_one = (xfull * rms_one * g_one).astype(bf16)
+    projected = mm("td,dc->tc", xn_one, w_qkv).reshape(length, 3, heads, HD)
+    cosine, sine = rotary(length, HD)
+    queries = rotate(projected[:, 0], cosine, sine).astype(bf16)
+    keys_all = rotate(projected[:, 1], cosine, sine).astype(bf16)
+    values_all = projected[:, 2].astype(bf16)
+    mixed, log_totals = attend_forward(queries, keys_all, values_all, segment, scale)
+    hidden_state = xfull + add_cores(mm("th,dh->td", mixed, w_out_t))
+    rms_two = rms_scale(hidden_state)
+    xn_two = (hidden_state * rms_two * g_two).astype(bf16)
+    logits = jnp.dot(xn_two, w_router, preferred_element_type=f32)
+    probs = jax.nn.softmax(logits, axis=-1)
+    match = (expert_ids[:, :, None] == jnp.arange(experts, dtype=jnp.int32)).astype(f32)
+    gates = jnp.sum(match * probs[:, None, :], axis=2) * kept_float
+
+    slot_gate = sum(
+        jnp.sum(jnp.where(slot[:, r : r + 1] == slots[None, :], gates[:, r : r + 1], 0.0), axis=0)
+        for r in range(top)
+    )
+    both = jnp.concatenate([xn_two, cotangent], axis=1)
+    placed = mm("ts,td->sd", pick_any, both)
+    placed = jnp.concatenate(
+        [placed[:, :width], placed[:, width:] * slot_gate[:, None]], axis=1
+    ).astype(bf16)
+    arrived = to_members(planes, placed.reshape(experts, capacity, 2 * width))
+    arrived = arrived.reshape(experts * capacity, 2 * width)
+    xin, dye = arrived[:, :width], arrived[:, width:]
+
+    shared_both = mm("td,df->tf", xn_two, s_gate_up).reshape(length, 2, s_hidden)
+    shared_hidden = silu_forward(shared_both)
+    shared_out = mm("tf,df->td", shared_hidden, s_down_t)
+    grad_shared_hidden = mm("td,df->tf", cotangent, s_down_t)
+    grad_s_down_t = mm("td,tf->df", cotangent, shared_hidden)
+    grad_shared_both = silu_back(shared_both, grad_shared_hidden).reshape(length, -1)
+    grad_s_gate_up = mm("td,tf->df", xn_two, grad_shared_both)
+    grad_xn_shared = mm("tf,df->td", grad_shared_both, s_gate_up)
+
+    both_parts = mm("sd,df->sf", xin, w_gate_up).reshape(-1, 2, hidden)
+    expert_hidden = silu_forward(both_parts)
+    expert_out = mm("sf,df->sd", expert_hidden, w_down_t).astype(bf16)
+    grad_hidden_expert = mm("sd,df->sf", dye, w_down_t)
+    grad_both = silu_back(both_parts, grad_hidden_expert).reshape(-1, 2 * hidden)
+    grad_in = mm("sf,df->sd", grad_both, w_gate_up).astype(bf16)
+    grad_down_t = mm("sd,sf->df", dye, expert_hidden)
+    grad_gate_up = mm("sd,sf->df", xin, grad_both)
+    back = jnp.concatenate([expert_out, grad_in], axis=1).reshape(experts, capacity, 2 * width)
+    back = to_members(planes, back).reshape(experts * capacity, 2 * width)
+    picked = [mm("ts,sd->td", pick[r], back[:, :width]) for r in range(top)]
+    moe = sum(gates[:, r : r + 1] * picked[r] for r in range(top))
+    grad_xn_moe = mm("ts,sd->td", pick_any, back[:, width:])
+    grad_y = cotangent.astype(f32)
+    grad_gates_part = kept_float * jnp.stack(
+        [jnp.sum(grad_y * picked[r], axis=-1) for r in range(top)], axis=1
+    )
+    ffn_part = (moe + shared_out).astype(bf16)
+    output = (
+        hidden_state + (ffn_part.astype(f32) + other_core(ffn_part).astype(f32))
+    ).astype(bf16)
+    grad_xn_sum = add_cores(grad_xn_shared + grad_xn_moe)
+    grad_gates = add_cores(grad_gates_part)
+
+    grad_probs = jnp.sum(match * grad_gates[:, :, None], axis=1)
+    grad_logits = (
+        probs * (grad_probs - jnp.sum(probs * grad_probs, axis=-1, keepdims=True))
+    ).astype(bf16)
+    grad_w_router = mm("td,te->de", xn_two, grad_logits)
+    grad_xn_two = grad_xn_sum + mm("te,de->td", grad_logits, w_router)
+    grad_norm_two, grad_g_two = norm_back(grad_xn_two, hidden_state, rms_two, g_two)
+    grad_hidden = grad_y + grad_norm_two
+    grad_attn = grad_hidden.astype(bf16)
+    grad_out_t = mm("td,th->dh", grad_attn, mixed)
+    grad_mixed = mm("td,dh->th", grad_attn, w_out_t).astype(bf16)
+    grad_queries, grad_keys, grad_values = attend_backward(
+        queries, keys_all, values_all, segment, scale, grad_mixed, log_totals
+    )
+    grad_projected = (
+        jnp.stack(
+            [rotate(grad_queries, cosine, -sine), rotate(grad_keys, cosine, -sine), grad_values],
+            axis=1,
+        )
+        .astype(bf16)
+        .reshape(length, 3 * heads_width)
+    )
+    grad_w_qkv = mm("td,tc->dc", xn_one, grad_projected)
+    xn_part = mm("tc,dc->td", grad_projected, w_qkv).astype(bf16)
+    grad_xn_one = xn_part.astype(f32) + other_core(xn_part).astype(f32)
+    grad_norm_one, grad_g_one = norm_back(grad_xn_one, xfull, rms_one, g_one)
+    grad_tokens = grad_hidden + grad_norm_one
+
+    small_grad = jnp.concatenate(
+        [grad_g_one[:, None], grad_g_two[:, None], grad_w_router], axis=1
+    )
+    small_grad = jnp.pad(small_grad, ((0, 0), (0, 128 - small_grad.shape[1])))
+    shared_grads = jnp.concatenate(
+        [
+            g.astype(bf16)
+            for g in (grad_s_gate_up, grad_s_down_t, grad_w_qkv, grad_out_t, small_grad)
+        ],
+        axis=1,
+    ).reshape(n, rows, -1)
+    expert_grads = jnp.concatenate(
+        [grad_gate_up.astype(bf16), grad_down_t.astype(bf16)], axis=1
+    ).reshape(n, rows, -1)
+    mine, mine_expert = reduce_grads(planes, shared_grads, expert_grads)
+    small_mine = part(mine, 4)
+    return (
+        output,
+        grad_tokens,
+        small_mine[:, 0],
+        part(mine, 2).reshape(rows, 3, heads_width),
+        part(mine, 3).T,
+        small_mine[:, 1],
+        small_mine[:, 2 : 2 + experts],
+        mine_expert[:, :, : 2 * hidden].reshape(experts, rows, 2, hidden),
+        mine_expert[:, :, 2 * hidden :].transpose(0, 2, 1),
+        part(mine, 0).reshape(rows, 2, s_hidden),
+        part(mine, 1).T,
+    )
+
+
 def solution(mesh):
+    def pick(*args):
+        experts, rows = args[9].shape[0], args[5].shape[0]
+        if experts == GROUP and mesh.shape["dp"] % GROUP == 0 and rows % 16 == 0:
+            return local_grouped(mesh.shape["dp"] // GROUP, *args)
+        return local_plain(*args)
+
     return jax.shard_map(
-        local,
+        pick,
         mesh=mesh,
         in_specs=(
             P("dp", None),

time: 1900 us -> 467 us (0.25)
  waiting for transfers between devices: 1460 us -> 41 us
  Pallas kernels: 0 us -> 269 us
  blocking collectives: 159 us -> 0 us
  local copies, waits for them, and re-layouts: 96.4 us -> 32.7 us
  matrix products: 110 us -> 80.7 us
  other arithmetic: 48.2 us -> 24.4 us
    reduce_scatter x8 -> x0, waiting for transfers between devices: 1050 us -> none  [the longest x1 326 us: local(): lax.psum_scatter(grad_w_gate_up, 'dp', scatter_dimension=1, tiled=True)]
    all_gather x7 -> x0, waiting for transfers between devices: 280 us -> none  [the longest x1 147 us: local(): lax.all_gather(gate_up, 'dp', axis=1, tiled=True)]
    pallas_call x0 -> x2, Pallas kernels: none -> 269 us  [the longest x1 160 us: reduce_grads(): pl.pallas_call(functools.partial(reduce_kernel, planes), out_shape=(jax.S...]
    unnamed x21 -> x0, waiting for transfers between devices: 136 us -> none
    all_gather x5 -> x0, blocking collectives: 82.1 us -> none  [the longest x1 40.4 us: local(): lax.all_gather(out_weight, 'dp', axis=1, tiled=True)]
    unnamed x3 -> x0, blocking collectives: 76.6 us -> none
    gather x16 -> x0, local copies, waits for them, and re-layouts: 50.9 us -> none  [the longest x2 10.5 us: local(): picked = expert_out[pair_slots]]
    ppermute x0 -> x11, waiting for transfers between devices: none -> 41 us  [the longest x6 40.3 us: to_members(): out.append(lax.ppermute(blocks[j], 'dp', order))]
  transfers between devices with their start and end apart: 18 -> 11, of which waited for: 13 -> 4; matrix products, arithmetic and copies ran while one was open for 10% -> 9% of each run, Pallas kernels for 0% -> 0%
where the time goes in v1:
time: 467 us; the launch traced here: 458 us
  Pallas kernels  269 us (58%)
  matrix products  80.7 us (17%)
  waiting for transfers between devices  41 us (9%)
  local copies, waits for them, and re-layouts  32.7 us (7%)
  other arithmetic  24.4 us (5%)
  starting transfers between devices  8.43 us (2%)
    pallas_call x1, Pallas kernels, reduce_grads(): pl.pallas_call(functools.partial(reduce_kernel, planes), out_shape=(jax.S...  160 us
    pallas_call x1, Pallas kernels, gather_weights(): pl.pallas_call(functools.partial(gather_kernel, planes), out_shape=(jax.S...  109 us
    dot_general x22, matrix products, mm(): return jnp.einsum(spec, a, b, preferred_element_type=f32)  63.1 us
    ppermute x6, waiting for transfers between devices, to_members(): out.append(lax.ppermute(blocks[j], 'dp', order))  40.3 us
  transfers between devices with their start and end apart: 11, of which 4 were waited for; matrix products, arithmetic and copies ran while one was open for 9% of the time, Pallas kernels for 0%

profile of v1, /device:TPU:8, one launch (start us, length us, event | category | flops | bytes accessed | tf_op | source)
XLA Modules:
  0.0 458.4 jit_solution(9618098905288083048)
XLA Ops:
  0.7 1.0 copy.163
  1.7 0.9 copy.162
  2.7 0.7 pad_maximum_fusion.16
  3.5 2.5 reshape.319
  6.1 1.1 pad_maximum_fusion.5.e_ref
  7.3 109.4 %shard_map.224 = (bf16[16,48,4736]{2,1,0:T(8,128)(2,1)}, bf16[16,48,3072]{2,1,0:T(8,128)(2,1)}) custom-call(bf16[48,4736]{1,0:T(8,128)(2,1)} %copy-done.12, bf16[4,48,3072]{2,1,0:T(8,128)(2,1)} %pad_maximum_fusion.5.e_ref), custom_call_target="tpu_custom_call" | custom-call | tf_op jit(solution)/shard_map/pallas_call | solution.py:569
  116.7 1.1 fusion.124
  118.8 2.7 fusion.49
  122.5 0.9 fusion.117
  124.0 1.2 fusion.127
  125.3 0.9 fusion
  126.2 1.7 copy-done
  127.9 1.1 fusion.76
  129.1 1.7 fusion.101
  131.3 1.3 convert_reduce_fusion
  133.6 0.7 collective-permute-done
  134.4 2.2 multiply_reduce_fusion.3
  138.0 1.6 fusion.128
  139.6 3.8 fusion.11
  143.5 2.1 fusion.43
  147.7 1.5 collective-permute-start.2
  149.2 1.4 collective-permute-start.3
  150.6 1.8 fusion.91
  152.6 3.6 fusion.3
  156.3 2.3 bitcast_dynamic-update-slice_fusion
  158.5 13.7 %fusion.9 = f32[512,768]{1,0:T(8,128)} fusion(bf16[512,2048]{0,1:T(8,128)(2,1)S(1)} %bitcast.184, bf16[768,4736]{1,0:T(8,128)(2,1)S(1)} %bitcast.209), kind=kOutput, calls=%fused_computation.48 | convolution fusion | flops 1610612736 | bytes 6815744 | tf_op jit(solution)/shard_map/tf,df->td/dot_general | solution.py:882
  172.3 11.6 %collective-permute-done.2 = bf16[256,1536]{1,0:T(8,128)(2,1)S(1)} collective-permute-done((bf16[256,1536]{1,0:T(8,128)(2,1)S(1)}, bf16[256,1536]{1,0:T(8,128)(2,1)S(1)}, u32[]{:S(2)}, u32[]{:S(2)}) %collective-permute-start.2) | collective-permute-done | bytes 786464 | tf_op jit(solution)/shard_map/ppermute | solution.py:820
  184.3 3.6 fusion.15
  187.9 4.9 %fusion.26 = (bf16[1024,1,1024]{0,2,1:T(8,128)(2,1)S(1)}, bf16[1024,1,1024]{0,2,1:T(8,128)(2,1)S(1)}, bf16[1024,1024]{0,1:T(8,128)(2,1)}) fusion(f32[1024,2,1024]{0,2,1:T(8,128)S(1)} %bitcast.241, bf16[768,3072]{1,0:T(8,128)(2,1)S(1)} %bitcast.238, bf16[1024,1536]{1,0:T(8,128)(2,1)S(1)} %bitcast.174), kind=kOutput, calls=%fused_computation.79 | convolution fusion | flops 1627389952 | bytes 17825792 | tf_op jit(solution)/shard_map/sd,df->sf/dot_general | solution.py:882
  193.2 3.7 convolution_convert_fusion.1
  196.9 3.4 fusion.27
  200.3 1.8 convolution_convert_fusion.4
  202.4 1.5 collective-permute-start.4
  204.5 1.4 collective-permute-start.6
  205.9 1.8 convolution_convert_fusion.5
  207.8 2.6 pad_maximum_fusion
  210.3 12.6 %collective-permute-done.4 = bf16[256,1536]{0,1:T(8,128)(2,1)S(1)} collective-permute-done((bf16[256,1536]{0,1:T(8,128)(2,1)S(1)}, bf16[256,1536]{0,1:T(8,128)(2,1)S(1)}, u32[]{:S(2)}, u32[]{:S(2)}) %collective-permute-start.4) | collective-permute-done | bytes 786464 | tf_op jit(solution)/shard_map/ppermute | solution.py:820
  222.9 16.1 %collective-permute-done.5 = bf16[256,1536]{0,1:T(8,128)(2,1)S(1)} collective-permute-done((bf16[256,1536]{0,1:T(8,128)(2,1)S(1)}, bf16[256,1536]{0,1:T(8,128)(2,1)S(1)}, u32[]{:S(2)}, u32[]{:S(2)}) %collective-permute-start.5) | collective-permute-done | bytes 786464 | tf_op jit(solution)/shard_map/ppermute | solution.py:820
  239.0 1.9 pad_maximum_fusion.3
  240.9 5.1 %copy.139 = bf16[4,256,1536]{2,1,0:T(8,128)(2,1)} copy(bf16[4,256,1536]{1,2,0:T(8,128)(2,1)} %pad_maximum_fusion.3) | data formatting | bytes 6291456 | tf_op jit(solution)/shard_map/stack | solution.py:821
  246.1 3.3 fusion.51
  249.5 1.1 fusion.21
  250.6 1.3 fusion.30
  252.5 2.6 add_convert_fusion.1
  255.4 2.5 multiply_reduce_fusion.1
  257.9 1.5 convert_add_fusion.1
  259.4 1.6 convolution_convert_fusion.7
  261.1 2.4 multiply_reduce_fusion
  263.4 1.9 multiply_convert_fusion
  265.3 2.1 fusion.71
  268.2 1.1 fusion.77
  270.1 2.8 fusion.55
  273.7 2.8 fusion.2
  276.5 1.5 fusion.70
  278.0 0.8 fusion.40
  279.1 0.8 pad_dynamic-update-slice_fusion
  279.9 159.6 %shard_map.225 = (f32[48,4736]{1,0:T(8,128)}, f32[4,48,3072]{2,1,0:T(8,128)}) custom-call(bf16[16,48,4736]{2,1,0:T(8,128)(2,1)} %bitcast.52.s_ref, bf16[16,48,3072]{2,1,0:T(8,128)(2,1)} %bitcast.168), custom_call_target="tpu_custom_call" | custom-call | tf_op jit(solution)/shard_map/pallas_call | solution.py:775
  439.4 2.8 slice.233
  442.2 2.1 slice_bitcast_fusion.6
  447.8 3.5 reshape.331
  451.2 1.1 reshape.332
  452.3 1.6 copy.165
  454.0 1.4 copy.149
  455.4 2.8 fusion.37
  (216 shorter events, 16.4 us)
Async XLA Ops:
  0.6 5.4 %copy-start.27 = (bf16[1024,48]{0,1:T(8,128)(2,1)S(1)}, bf16[1024,48]{0,1:T(8,128)(2,1)}, u32[]{:S(2)}) copy-start(bf16[1024,48]{0,1:T(8,128)(2,1)} %param.26) | copy-start | bytes 294916
  0.7 5.4 %copy-start.41 = (bf16[384,48]{0,1:T(8,128)(2,1)S(1)}, bf16[384,48]{0,1:T(8,128)(2,1)}, u32[]{:S(2)}) copy-start(bf16[384,48]{0,1:T(8,128)(2,1)} %param.20) | copy-start | bytes 110596
  0.7 5.5 %copy-start.23 = (bf16[4,1024,48]{1,2,0:T(8,128)(2,1)S(1)}, bf16[4,1024,48]{1,2,0:T(8,128)(2,1)}, u32[]{:S(2)}) copy-start(bf16[4,1024,48]{1,2,0:T(8,128)(2,1)} %param.24) | copy-start | bytes 1179652
  6.1 111.9 %copy-start.1 = (bf16[512,768]{1,0:T(8,128)(2,1)S(1)}, bf16[512,768]{1,0:T(8,128)(2,1)}, u32[]{:S(2)}) copy-start(bf16[512,768]{1,0:T(8,128)(2,1)} %param.14) | copy-start | bytes 2359300
  118.0 3.5 copy-start.38
  118.8 2.7 copy-start.46
  121.5 4.7 %copy-start.10 = (f32[512,1152]{0,1:T(8,128)}, f32[512,1152]{0,1:T(8,128)S(1)}, u32[]{:S(2)}) copy-start(f32[512,1152]{0,1:T(8,128)S(1)} %fusion.49) | copy-start | bytes 7077892
  125.3 2.6 copy-start
  129.0 1.9 copy-start.33
  129.1 2.3 copy-start.49
  130.8 2.9 copy-start.5
  130.8 3.6 collective-permute-start
  133.0 4.2 copy-start.31
  133.0 12.8 %copy-start.54 = (s32[512,1]{0,1:T(1,128)}, s32[512,1]{0,1:T(1,128)S(1)}, u32[]{:S(2)}) copy-start(s32[512,1]{0,1:T(1,128)S(1)} %get-tuple-element.176) | copy-start | bytes 6148
  138.0 14.7 %copy-start.3 = (bf16[512,768]{1,0:T(8,128)(2,1)}, bf16[512,768]{1,0:T(8,128)(2,1)S(1)}, u32[]{:S(2)}) copy-start(bf16[512,768]{1,0:T(8,128)(2,1)S(1)} %multiply_convert_fusion.5) | copy-start | bytes 2359300
  139.6 3.9 copy-start.28
  139.6 4.0 copy-start.19
  143.4 2.2 copy-start.35
  143.5 2.4 copy-start.56
  143.5 2.4 copy-start.58
  145.6 4.9 %slice-start.2 = ((s8[7274496]{0:T(1024)(128)(4,1)}), s8[4194304]{0:T(1024)(128)(4,1)S(1)}, s32[]{:S(2)}) async-start(s8[7274496]{0:T(1024)(128)(4,1)} %bitcast.206), calls=%async_computation.2 | async-start | bytes 8388608
  146.5 4.1 slice-start.3
  147.0 25.2 %collective-permute-start.1 = (bf16[256,1536]{1,0:T(8,128)(2,1)S(1)}, bf16[256,1536]{1,0:T(8,128)(2,1)S(1)}, u32[]{:S(2)}, u32[]{:S(2)}) collective-permute-start(bf16[256,1536]{1,0:T(8,128)(2,1)S(1)} %get-tuple-element.154), channel_id=1, source_target_pairs={{0,2},{2,0},{4,6},{6,4},{8,10},{10,8},{12,14},{14,12},{16,18},{18,... | collective-permute-start | bytes 2359304 | tf_op jit(solution)/shard_map/ppermute | solution.py:820
  147.7 36.2 %collective-permute-start.2 = (bf16[256,1536]{1,0:T(8,128)(2,1)S(1)}, bf16[256,1536]{1,0:T(8,128)(2,1)S(1)}, u32[]{:S(2)}, u32[]{:S(2)}) collective-permute-start(bf16[256,1536]{1,0:T(8,128)(2,1)S(1)} %get-tuple-element.156), channel_id=1, source_target_pairs={{0,4},{2,6},{4,0},{6,2},{8,12},{10,14},{12,8},{14,10},{16,20},{18,... | collective-permute-start | bytes 2359304 | tf_op jit(solution)/shard_map/ppermute | solution.py:820
  149.2 34.6 %collective-permute-start.3 = (bf16[256,1536]{1,0:T(8,128)(2,1)S(1)}, bf16[256,1536]{1,0:T(8,128)(2,1)S(1)}, u32[]{:S(2)}, u32[]{:S(2)}) collective-permute-start(bf16[256,1536]{1,0:T(8,128)(2,1)S(1)} %get-tuple-element.155), channel_id=1, source_target_pairs={{0,6},{2,4},{4,2},{6,0},{8,14},{10,12},{12,10},{14,8},{16,22},{18,... | collective-permute-start | bytes 2359304 | tf_op jit(solution)/shard_map/ppermute | solution.py:820
  152.4 3.8 copy-start.60
  156.2 28.0 %slice-start.4 = ((s8[4718592]{0:T(1024)(128)(4,1)}), s8[4194304]{0:T(1024)(128)(4,1)S(1)}, s32[]{:S(2)}) async-start(s8[4718592]{0:T(1024)(128)(4,1)} %bitcast.235), calls=%async_computation.4 | async-start | bytes 8388608
  158.5 25.8 %slice-start.5 = ((s8[4718592]{0:T(1024)(128)(4,1)}), s8[524288]{0:T(1024)(128)(4,1)S(1)}, s32[]{:S(2)}) async-start(s8[4718592]{0:T(1024)(128)(4,1)} %bitcast.235), calls=%async_computation.5 | async-start | bytes 1048576
  196.9 3.4 copy-start.62
  202.4 20.5 %collective-permute-start.4 = (bf16[256,1536]{0,1:T(8,128)(2,1)S(1)}, bf16[256,1536]{0,1:T(8,128)(2,1)S(1)}, u32[]{:S(2)}, u32[]{:S(2)}) collective-permute-start(bf16[256,1536]{0,1:T(8,128)(2,1)S(1)} %get-tuple-element.150), channel_id=1, source_target_pairs={{0,2},{2,0},{4,6},{6,4},{8,10},{10,8},{12,14},{14,12},{16,18},{18,... | collective-permute-start | bytes 2359304 | tf_op jit(solution)/shard_map/ppermute | solution.py:820
  203.8 35.2 %collective-permute-start.5 = (bf16[256,1536]{0,1:T(8,128)(2,1)S(1)}, bf16[256,1536]{0,1:T(8,128)(2,1)S(1)}, u32[]{:S(2)}, u32[]{:S(2)}) collective-permute-start(bf16[256,1536]{0,1:T(8,128)(2,1)S(1)} %get-tuple-element.152), channel_id=1, source_target_pairs={{0,4},{2,6},{4,0},{6,2},{8,12},{10,14},{12,8},{14,10},{16,20},{18,... | collective-permute-start | bytes 2359304 | tf_op jit(solution)/shard_map/ppermute | solution.py:820
  204.5 34.6 %collective-permute-start.6 = (bf16[256,1536]{0,1:T(8,128)(2,1)S(1)}, bf16[256,1536]{0,1:T(8,128)(2,1)S(1)}, u32[]{:S(2)}, u32[]{:S(2)}) collective-permute-start(bf16[256,1536]{0,1:T(8,128)(2,1)S(1)} %get-tuple-element.151), channel_id=1, source_target_pairs={{0,6},{2,4},{4,2},{6,0},{8,14},{10,12},{12,10},{14,8},{16,22},{18,... | collective-permute-start | bytes 2359304 | tf_op jit(solution)/shard_map/ppermute | solution.py:820
  246.1 3.4 copy-start.6
  246.1 3.4 copy-start.55
  249.4 6.0 %collective-permute-start.8 = (f32[512,768]{1,0:T(8,128)S(1)}, f32[512,768]{1,0:T(8,128)S(1)}, u32[]{:S(2)}, u32[]{:S(2)}) collective-permute-start(f32[512,768]{1,0:T(8,128)S(1)} %fusion.51), channel_id=1, source_target_pairs={{0,1},{1,0},{2,3},{3,2},{4,5},{5,4},{6,7},{7,6},{8,9},{9,8},{10,11... | collective-permute-start | bytes 4718600 | tf_op jit(solution)/shard_map/ppermute | solution.py:809
  250.6 1.9 copy-start.57
  251.9 3.3 collective-permute-start.9
  252.5 2.8 copy-start.34
  252.5 2.8 copy-start.29
  252.5 2.8 copy-start.36
  252.5 2.8 copy-start.32
  252.5 2.8 copy-start.43
  255.1 2.8 collective-permute-start.7
  255.3 2.6 copy-start.44
  255.3 2.6 copy-start.53
  255.4 5.7 %slice-start = ((s8[6291456]{0:T(1024)(128)(4,1)}), s8[4194304]{0:T(1024)(128)(4,1)S(1)}, s32[]{:S(2)}) async-start(s8[6291456]{0:T(1024)(128)(4,1)} %bitcast.166), calls=%async_computation | async-start | bytes 8388608
  257.9 3.1 slice-start.1
  265.3 2.2 copy-start.14
  265.3 2.2 copy-start.16
  270.0 3.4 copy-start.4
  270.0 3.4 copy-start.30
  270.0 3.4 copy-start.37
  270.0 3.4 copy-start.45
  270.0 3.6 copy-start.51
  270.0 3.6 copy-start.2
  270.0 3.6 copy-start.39
  270.1 3.6 copy-start.47
  272.9 5.1 %copy-start.7 = (bf16[512,768]{1,0:T(8,128)(2,1)}, bf16[512,768]{1,0:T(8,128)(2,1)S(1)}, u32[]{:S(2)}) copy-start(bf16[512,768]{1,0:T(8,128)(2,1)S(1)} %fusion.55) | copy-start | bytes 2359300
  272.9 5.1 %collective-permute-start.10 = (bf16[512,768]{1,0:T(8,128)(2,1)S(1)}, bf16[512,768]{1,0:T(8,128)(2,1)S(1)}, u32[]{:S(2)}, u32[]{:S(2)}) collective-permute-start(bf16[512,768]{1,0:T(8,128)(2,1)S(1)} %fusion.55), channel_id=1, source_target_pairs={{0,1},{1,0},{2,3},{3,2},{4,5},{5,4},{6,7},{7,6},{8,9},{9,8},{10,11... | collective-permute-start | bytes 2359304 | tf_op jit(solution)/shard_map/ppermute | solution.py:809
  439.4 4.9 %copy-start.11 = (f32[48,4736]{1,0:T(8,128)S(1)}, f32[48,4736]{1,0:T(8,128)}, u32[]{:S(2)}) copy-start(f32[48,4736]{1,0:T(8,128)} %get-tuple-element.63) | copy-start | bytes 2727940
  447.8 7.6 %copy-start.8 = (bf16[512,768]{1,0:T(8,128)(2,1)S(1)}, bf16[512,768]{1,0:T(8,128)(2,1)}, u32[]{:S(2)}) copy-start(bf16[512,768]{1,0:T(8,128)(2,1)} %copy-done.7) | copy-start | bytes 2359300
  447.8 7.6 %copy-start.40 = (f32[768]{0:T(1024)S(1)}, f32[768]{0:T(1024)}, u32[]{:S(2)}) copy-start(f32[768]{0:T(1024)} %copy-done.38) | copy-start | bytes 9220
  447.8 7.6 %copy-start.48 = (f32[512]{0:T(512)S(1)}, f32[512]{0:T(512)}, u32[]{:S(2)}) copy-start(f32[512]{0:T(512)} %copy-done.46) | copy-start | bytes 6148
  447.8 7.6 %copy-start.50 = (f32[512]{0:T(512)S(1)}, f32[512]{0:T(512)}, u32[]{:S(2)}) copy-start(f32[512]{0:T(512)} %get-tuple-element.180) | copy-start | bytes 6148
  (16 other events, 20.0 us)

commit v2 on v1

--- a/solution.py
+++ b/solution.py
@@ -421,6 +421,9 @@
     def down(self):
         return (self.d - GROUP, self.c)
 
+    def twin(self):
+        return (self.d, 1 - self.c)
+
     def when(self, condition, action):
         pl.when(condition)(action)
 
@@ -436,12 +439,13 @@
         def hello(device):
             pl.semaphore_signal(barrier, inc=1, device_id=device, device_id_type=MESH)
 
+        hello(self.twin())
         for j in range(1, GROUP):
             hello(self.near(j))
         self.when(self.has_up(), lambda: hello(self.up()))
         self.when(self.has_down(), lambda: hello(self.down()))
         line = self.has_up().astype(jnp.int32) + self.has_down().astype(jnp.int32)
-        pl.semaphore_wait(barrier, GROUP - 1 + line)
+        pl.semaphore_wait(barrier, GROUP + line)
 
 
 def send(source, target, send_sem, recv_sem, device):
@@ -455,134 +459,465 @@
     )
 
 
-def gather_kernel(planes, s_ref, e_ref, s_all, e_all, local_sem, s_recv, e_recv, s_send, e_send):
+class Everywhere:
+    def __init__(self, at, own, all_blocks, local_sem, recvs, sends):
+        self.at, self.own, self.all = at, own, all_blocks
+        self.local_sem, self.recvs, self.sends = local_sem, recvs, sends
+
+    def copy(self, block, source, way, device):
+        return send(source, self.all.at[block], self.sends.at[way, block], self.recvs.at[block], device)
+
+    def keep(self):
+        return pltpu.make_async_copy(self.own, self.all.at[self.at.d], self.local_sem)
+
+    def landed(self, block):
+        self.copy(block, self.own, 0, self.at.near(1)).wait_recv()
+
+    def start_line(self):
+        at = self.at
+        at.when(at.has_up(), lambda: self.copy(at.d, self.own, 0, at.up()).start())
+        at.when(at.has_down(), lambda: self.copy(at.d, self.own, 1, at.down()).start())
+
+    def start_plane(self):
+        at = self.at
+        self.copy(at.d, self.own, 2, at.near(1)).start()
+        self.copy(at.d, self.own, 3, at.near(2)).start()
+        self.keep().start()
+
+    def spread(self, k):
+        at = self.at
+
+        def go(plane, more, way, device_of):
+            block = plane * GROUP + at.p
+            source = self.all.at[block]
+            self.landed(block)
+            at.when(more, lambda: self.copy(block, source, way, device_of()).start())
+            self.copy(block, source, 2, at.near(1)).start()
+            self.copy(block, source, 3, at.near(2)).start()
+
+        at.when(at.has_down(k), lambda: go(at.z - k, at.has_up(), 0, at.up))
+        at.when(at.has_up(k), lambda: go(at.z + k, at.has_down(), 1, at.down))
+
+    def cross(self, k):
+        at = self.at
+
+        def go(plane):
+            first = plane * GROUP + at.member[1]
+            second = plane * GROUP + at.member[2]
+            even = lax.rem(plane, 2) == 0
+            self.landed(first)
+            at.when(even, lambda: self.copy(first, self.all.at[first], 3, at.near(2)).start())
+            self.landed(second)
+            at.when(
+                jnp.logical_not(even),
+                lambda: self.copy(second, self.all.at[second], 2, at.near(1)).start(),
+            )
+
+        if k == 0:
+            go(at.z)
+        else:
+            at.when(at.has_down(k), lambda: go(at.z - k))
+            at.when(at.has_up(k), lambda: go(at.z + k))
+
+    def diagonal(self):
+        for plane in range(self.at.planes):
+            self.landed(plane * GROUP + self.at.member[3])
+        self.keep().wait()
+
+    def sent(self):
+        at = self.at
+        for plane in range(at.planes):
+            block = plane * GROUP + at.p
+            self.copy(block, self.own, 2, at.near(1)).wait_send()
+            self.copy(block, self.own, 3, at.near(2)).wait_send()
+            if plane % 2 == 0:
+                self.copy(plane * GROUP + at.member[1], self.own, 3, at.near(2)).wait_send()
+            else:
+                self.copy(plane * GROUP + at.member[2], self.own, 2, at.near(1)).wait_send()
+
+            def gone(way, device_of):
+                self.copy(block, self.own, way, device_of()).wait_send()
+
+            at.when((at.z >= plane) & at.has_up(), lambda: gone(0, at.up))
+            at.when((at.z <= plane) & at.has_down(), lambda: gone(1, at.down))
+
+
+class Experts:
+    def __init__(self, at, own, all_blocks, local_sem, recvs, sends):
+        self.at, self.own, self.all = at, own, all_blocks
+        self.local_sem, self.recvs, self.sends = local_sem, recvs, sends
+
+    def line(self, block, source, way, device):
+        return send(source, self.all.at[block], self.sends.at[way, block], self.recvs.at[block], device)
+
+    def across(self, j):
+        at = self.at
+        return send(
+            self.own.at[at.member[j]],
+            self.all.at[at.d],
+            self.sends.at[1 + j, at.d],
+            self.recvs.at[at.d],
+            at.near(j),
+        )
+
+    def keep(self):
+        return pltpu.make_async_copy(self.own.at[self.at.p], self.all.at[self.at.d], self.local_sem)
+
+    def start_plane(self):
+        for j in range(1, GROUP):
+            self.across(j).start()
+        self.keep().start()
+
+    def start_line(self):
+        at = self.at
+        source = self.own.at[at.p]
+        at.when(at.has_up(), lambda: self.line(at.d, source, 0, at.up()).start())
+        at.when(at.has_down(), lambda: self.line(at.d, source, 1, at.down()).start())
+
+    def landed(self, block):
+        self.line(block, self.own.at[0], 0, self.at.near(1)).wait_recv()
+
+    def plane_step(self, j):
+        at = self.at
+        block = at.z * GROUP + at.member[j]
+        source = self.all.at[block]
+        self.landed(block)
+        at.when(at.has_up(), lambda: self.line(block, source, 0, at.up()).start())
+        at.when(at.has_down(), lambda: self.line(block, source, 1, at.down()).start())
+
+    def line_step(self, k, j):
+        at = self.at
+
+        def go(plane, more, way, device_of):
+            block = plane * GROUP + at.member[j]
+            self.landed(block)
+            at.when(more, lambda: self.line(block, self.all.at[block], way, device_of()).start())
+
+        at.when(at.has_down(k), lambda: go(at.z - k, at.has_up(), 0, at.up))
+        at.when(at.has_up(k), lambda: go(at.z + k, at.has_down(), 1, at.down))
+
+    def sent(self):
+        at = self.at
+        self.keep().wait()
+        for j in range(1, GROUP):
+            self.across(j).wait_send()
+        for plane in range(at.planes):
+
+            def gone(way, device_of):
+                for q in range(GROUP):
+                    self.line(plane * GROUP + q, self.own.at[0], way, device_of()).wait_send()
+
+            at.when((at.z >= plane) & at.has_up(), lambda: gone(0, at.up))
+            at.when((at.z <= plane) & at.has_down(), lambda: gone(1, at.down))
+
+
+def dot_nn(a, b):
+    return jnp.dot(a, b, preferred_element_type=jnp.float32)
+
+
+def dot_nt(a, b):
+    return lax.dot_general(a, b, (((1,), (1,)), ((), ())), preferred_element_type=jnp.float32)
+
+
+def dot_tn(a, b):
+    return lax.dot_general(a, b, (((0,), (0,)), ((), ())), preferred_element_type=jnp.float32)
+
+
+def lanes(count=128):
+    return lax.broadcasted_iota(jnp.int32, (1, count), 1)
+
+
+def turn(values, cosine, sine):
+    half = HD // 2
+    other = jnp.where(
+        lax.rem(lanes(), HD) < half,
+        -pltpu.roll(values, 2 * HD - half, 1),
+        pltpu.roll(values, half, 1),
+    )
+    return values * cosine + other * sine
+
+
+def blocks_of(ref, start, stop):
+    block = ref[:, :, start:stop]
+    return block.reshape(block.shape[0] * block.shape[1], stop - start)
+
+
+def attention_blocks(length):
+    size = length // 2
+    return [(i * size, (i + 1) * size) for i in range(2)]
+
+
+def forward_kernel(
+    planes,
+    experts,
+    x_ref,
+    cot_ref,
+    seg_col,
+    seg_row,
+    ids_ref,
+    order_ref,
+    ids_t_ref,
+    order_t_ref,
+    cos_ref,
+    sin_ref,
+    a_own,
+    s_own,
+    e_own,
+    a_all,
+    s_all,
+    e_all,
+    q_ref,
+    k_ref,
+    v_ref,
+    o_ref,
+    lse_ref,
+    h_ref,
+    xa_ref,
+    xf_ref,
+    probs_ref,
+    pair_ref,
+    placed_ref,
+    arrived_ref,
+    bias_ref,
+    mine_ref,
+    theirs_ref,
+    local_sem,
+    a_recv,
+    a_send,
+    s_recv,
+    s_send,
+    e_recv,
+    e_send,
+    twin_sem,
+    token_recv,
+    token_send,
+):
+    f32, bf16 = jnp.float32, jnp.bfloat16
     at = Place(planes)
-    own = at.d
-
-    def s_copy(block, source, way, device):
-        return send(source, s_all.at[block], s_send.at[way, block], s_recv.at[block], device)
-
-    def e_copy(block, source, way, device):
-        return send(source, e_all.at[block], e_send.at[way, block], e_recv.at[block], device)
-
-    def s_landed(block):
-        s_copy(block, s_ref, 0, at.near(1)).wait_recv()
-
-    def e_landed(block):
-        e_copy(block, e_ref.at[0], 0, at.near(1)).wait_recv()
+    length, width = x_ref.shape
+    heads_width = q_ref.shape[1]
+    capacity = length * ids_ref.shape[1] // experts
+    half = capacity // 2
+    attn = Everywhere(at, a_own, a_all, local_sem.at[0], a_recv, a_send)
+    shared = Everywhere(at, s_own, s_all, local_sem.at[1], s_recv, s_send)
+    expert = Experts(at, e_own, e_all, local_sem.at[2], e_recv, e_send)
 
     at.greet()
-    keep_s = pltpu.make_async_copy(s_ref, s_all.at[own], local_sem.at[0])
-    keep_e = pltpu.make_async_copy(e_ref.at[at.p], e_all.at[own], local_sem.at[1])
-    keep_s.start()
-    keep_e.start()
+    attn.start_line()
+    attn.start_plane()
+    expert.start_plane()
+    shared.start_line()
+    expert.start_line()
+
+    todo = []
     for j in range(1, GROUP):
-        send(
-            e_ref.at[at.member[j]],
-            e_all.at[own],
-            e_send.at[1 + j, own],
-            e_recv.at[own],
-            at.near(j),
-        ).start()
-    at.when(at.has_up(), lambda: s_copy(own, s_ref, 0, at.up()).start())
-    at.when(at.has_down(), lambda: s_copy(own, s_ref, 1, at.down()).start())
-    s_copy(own, s_ref, 2, at.near(1)).start()
-    s_copy(own, s_ref, 3, at.near(2)).start()
-    at.when(at.has_up(), lambda: e_copy(own, e_ref.at[at.p], 0, at.up()).start())
-    at.when(at.has_down(), lambda: e_copy(own, e_ref.at[at.p], 1, at.down()).start())
-
-    for j in range(1, GROUP):
-        block = at.z * GROUP + at.member[j]
-        e_landed(block)
-        at.when(at.has_up(), lambda: e_copy(block, e_all.at[block], 0, at.up()).start())
-        at.when(at.has_down(), lambda: e_copy(block, e_all.at[block], 1, at.down()).start())
-
-    def cross(plane):
-        first = plane * GROUP + at.member[1]
-        second = plane * GROUP + at.member[2]
-        even = lax.rem(plane, 2) == 0
-        s_landed(first)
-        at.when(even, lambda: s_copy(first, s_all.at[first], 3, at.near(2)).start())
-        s_landed(second)
-        at.when(
-            jnp.logical_not(even),
-            lambda: s_copy(second, s_all.at[second], 2, at.near(1)).start(),
+        todo.append(functools.partial(expert.plane_step, j))
+    todo.append(shared.start_plane)
+    for k in range(1, planes):
+        todo.append(functools.partial(shared.spread, k))
+        for j in range(GROUP):
+            todo.append(functools.partial(expert.line_step, k, j))
+        todo.append(functools.partial(shared.cross, k - 1))
+    todo.append(functools.partial(shared.cross, planes - 1))
+    todo.reverse()
+
+    def tick(count=1):
+        for _ in range(count):
+            if todo:
+                todo.pop()()
+
+    for start, stop in attention_blocks(length):
+        rows = lax.broadcasted_iota(jnp.int32, (stop - start, stop), 0) + start
+        columns = lax.broadcasted_iota(jnp.int32, (stop - start, stop), 1)
+        allowed = (columns <= rows) & (seg_col[start:stop, :] == seg_row[:, :stop])
+        bias_ref[start:stop, :stop] = jnp.where(allowed, 0.0, -1e30)
+
+    def slot_of(expert_id, position):
+        which = position // half
+        apart = which + at.c - 2 * which * at.c
+        bit0, bit1 = lax.rem(expert_id, 2), expert_id // 2
+        p0, p1 = lax.rem(at.p, 2), at.p // 2
+        distance = (bit0 + p0 - 2 * bit0 * p0) + 2 * (bit1 + p1 - 2 * bit1 * p1)
+        slot = apart * (experts * half) + distance * half + lax.rem(position, half)
+        return jnp.where(position < capacity, slot, -1)
+
+    slot_cols, slot_rows = [], []
+    top = ids_ref.shape[1]
+    for r in range(top):
+        count_col = jnp.zeros((length, 1), jnp.int32)
+        count_row = jnp.zeros((1, length), jnp.int32)
+        for other in range(top):
+            first = (ids_t_ref[other : other + 1, :] == ids_ref[:, r : r + 1]) & (
+                order_t_ref[other : other + 1, :] < order_ref[:, r : r + 1]
+            )
+            count_col += jnp.sum(first.astype(jnp.int32), axis=1, keepdims=True)
+            first = (ids_ref[:, other : other + 1] == ids_t_ref[r : r + 1, :]) & (
+                order_ref[:, other : other + 1] < order_t_ref[r : r + 1, :]
+            )
+            count_row += jnp.sum(first.astype(jnp.int32), axis=0, keepdims=True)
+        slot_cols.append(slot_of(ids_ref[:, r : r + 1], count_col))
+        slot_rows.append(slot_of(ids_t_ref[r : r + 1, :], count_row))
+
+    attn.spread(1)
+    attn.cross(0)
+    for k in range(2, planes):
+        attn.spread(k)
+        attn.cross(k - 1)
+        tick()
+    attn.cross(planes - 1)
+    attn.diagonal()
+
+    small = blocks_of(a_all, 4 * heads_width, 4 * heads_width + 128)
+    small_rows = small.astype(f32).T
+    g_one, g_two = small_rows[0:1, :], small_rows[1:2, :]
+    x = x_ref[...].astype(f32)
+    rms = lax.rsqrt(jnp.mean(x * x, axis=-1, keepdims=True) + epsilon)
+    xa_ref[...] = (x * rms * g_one).astype(bf16)
+    tick()
+    cosine, sine = cos_ref[...], sin_ref[...]
+    pairs = heads_width // 128
+    for i, ref in enumerate((q_ref, k_ref)):
+        part = dot_nn(xa_ref[...], blocks_of(a_all, i * heads_width, (i + 1) * heads_width))
+        for g in range(pairs):
+            columns = slice(128 * g, 128 * (g + 1))
+            ref[:, columns] = turn(part[:, columns], cosine, sine).astype(bf16)
+        tick()
+    v_ref[...] = dot_nn(
+        xa_ref[...], blocks_of(a_all, 2 * heads_width, 3 * heads_width)
+    ).astype(bf16)
+    tick()
+
+    scale = HD ** (-0.5)
+    for start, stop in attention_blocks(length):
+        logs = jnp.zeros((stop - start, 128), f32)
+        for g in range(pairs):
+            columns = slice(128 * g, 128 * (g + 1))
+            queries = q_ref[start:stop, columns]
+            keys, values = k_ref[:stop, columns], v_ref[:stop, columns]
+            mixed = []
+            for i in range(2):
+                one = jnp.where(lanes() // HD == i, queries, jnp.zeros_like(queries))
+                scores = dot_nt(one, keys) * scale + bias_ref[start:stop, :stop]
+                largest = jnp.max(scores, axis=-1, keepdims=True)
+                expo = jnp.exp(scores - largest)
+                total = jnp.sum(expo, axis=-1, keepdims=True)
+                weights = (expo * (1.0 / total)).astype(bf16)
+                mixed.append(dot_nn(weights, values))
+                logs = jnp.where(lanes() == 2 * g + i, largest + jnp.log(total), logs)
+            o_ref[start:stop, columns] = jnp.where(lanes() < HD, mixed[0], mixed[1]).astype(bf16)
+            tick(2)
+        lse_ref[start:stop, :] = logs
+
+    mine_ref[...] = dot_nt(o_ref[...], blocks_of(a_all, 3 * heads_width, 4 * heads_width))
+    swap = send(mine_ref, theirs_ref, twin_sem.at[0], twin_sem.at[1], at.twin())
+    swap.start()
+    tick(2)
+    swap.wait_recv()
+    h = x_ref[...].astype(f32) + (mine_ref[...] + theirs_ref[...])
+    h_ref[...] = h
+    rms = lax.rsqrt(jnp.mean(h * h, axis=-1, keepdims=True) + epsilon)
+    xf_ref[...] = (h * rms * g_two).astype(bf16)
+
+    is_expert = (lanes() >= 2) & (lanes() < 2 + experts)
+    logits = jnp.where(is_expert, dot_nn(xf_ref[...], small), -1e30)
+    expo = jnp.exp(logits - jnp.max(logits, axis=-1, keepdims=True))
+    probs = expo / jnp.sum(expo, axis=-1, keepdims=True)
+    probs_ref[...] = probs
+    packed = jnp.zeros((length, 128), f32)
+    for r in range(top):
+        chosen = lanes() == ids_ref[:, r : r + 1] + 2
+        gate = jnp.sum(jnp.where(chosen, probs, 0.0), axis=-1, keepdims=True)
+        gate = jnp.where(slot_cols[r] >= 0, gate, 0.0)
+        packed = jnp.where(lanes() == r, gate, packed)
+        packed = jnp.where(lanes() == top + r, slot_cols[r].astype(f32), packed)
+    pair_ref[...] = packed
+    gate_rows = packed.T
+    tick(2)
+
+    def outgoing(j):
+        return send(
+            placed_ref.at[j], arrived_ref.at[0, j], token_send.at[j], token_recv.at[j], at.near(j)
         )
 
-    def spread(plane, onward, device_of):
-        block = plane * GROUP + at.p
-        s_landed(block)
-        at.when(onward[0], lambda: s_copy(block, s_all.at[block], onward[1], device_of()).start())
-        s_copy(block, s_all.at[block], 2, at.near(1)).start()
-        s_copy(block, s_all.at[block], 3, at.near(2)).start()
-
-    def pass_on(plane, onward, device_of):
-        for j in range(GROUP):
-            block = plane * GROUP + at.member[j]
-            e_landed(block)
-            at.when(
-                onward[0], lambda: e_copy(block, e_all.at[block], onward[1], device_of()).start()
-            )
-
-    cross(at.z)
-    for k in range(1, planes):
-        below, above = at.z - k, at.z + k
-        at.when(at.has_down(k), lambda: spread(below, (at.has_up(), 0), at.up))
-        at.when(at.has_up(k), lambda: spread(above, (at.has_down(), 1), at.down))
-        at.when(at.has_down(k), lambda: pass_on(below, (at.has_up(), 0), at.up))
-        at.when(at.has_up(k), lambda: pass_on(above, (at.has_down(), 1), at.down))
-        at.when(at.has_down(k), lambda: cross(below))
-        at.when(at.has_up(k), lambda: cross(above))
-
-    keep_s.wait()
-    keep_e.wait()
-    for j in range(1, GROUP):
-        send(
-            e_ref.at[at.member[j]],
-            e_all.at[own],
-            e_send.at[1 + j, own],
-            e_recv.at[own],
-            at.near(j),
-        ).wait_send()
-    for plane in range(planes):
-        s_landed(plane * GROUP + at.member[3])
-        block = plane * GROUP + at.p
-        s_copy(block, s_ref, 2, at.near(1)).wait_send()
-        s_copy(block, s_ref, 3, at.near(2)).wait_send()
-        if plane % 2 == 0:
-            s_copy(plane * GROUP + at.member[1], s_ref, 3, at.near(2)).wait_send()
-        else:
-            s_copy(plane * GROUP + at.member[2], s_ref, 2, at.near(1)).wait_send()
-
-        def sent(way, device_of):
-            s_copy(block, s_ref, way, device_of()).wait_send()
-            for q in range(GROUP):
-                e_copy(plane * GROUP + q, e_ref.at[0], way, device_of()).wait_send()
-
-        at.when((at.z >= plane) & at.has_up(), lambda: sent(0, at.up))
-        at.when((at.z <= plane) & at.has_down(), lambda: sent(1, at.down))
-
-
-def gather_weights(planes, shared, expert):
+    for j in range(experts):
+        index = lax.broadcasted_iota(jnp.int32, (half, 1), 0) + j * half
+        pick = [slot_rows[r] == index for r in range(top)]
+        slot_gate = sum(
+            jnp.sum(jnp.where(pick[r], gate_rows[r : r + 1, :], 0.0), axis=1, keepdims=True)
+            for r in range(top)
+        )
+        pick = sum(p.astype(f32) for p in pick).astype(bf16)
+        target = arrived_ref.at[0, 0] if j == 0 else placed_ref.at[j]
+        target[:, :width] = dot_nn(pick, xf_ref[...]).astype(bf16)
+        target[:, width:] = (dot_nn(pick, cot_ref[...]) * slot_gate).astype(bf16)
+        if j:
+            outgoing(j).start()
+        tick()
+    for j in range(1, experts):
+        outgoing(j).wait_recv()
+        tick()
+    across = send(arrived_ref.at[0], arrived_ref.at[1], twin_sem.at[2], twin_sem.at[3], at.twin())
+    across.start()
+
+    tick(len(todo))
+    shared.diagonal()
+    across.wait_recv()
+    across.wait_send()
+    swap.wait_send()
+    for j in range(1, experts):
+        outgoing(j).wait_send()
+    attn.sent()
+    shared.sent()
+    expert.sent()
+
+
+def forward_pass(planes, experts, inputs, own, heads_width):
     n = planes * GROUP
-    anywhere = pl.BlockSpec(memory_space=pl.ANY)
+    bf16, f32, dma = jnp.bfloat16, jnp.float32, pltpu.SemaphoreType.DMA
+    length, width = inputs[0].shape
+    half = length * inputs[4].shape[1] // experts // 2
+    vmem, anywhere = pl.BlockSpec(memory_space=pltpu.VMEM), pl.BlockSpec(memory_space=pl.ANY)
+    shape = jax.ShapeDtypeStruct
     return pl.pallas_call(
-        functools.partial(gather_kernel, planes),
+        functools.partial(forward_kernel, planes, experts),
         out_shape=(
-            jax.ShapeDtypeStruct((n,) + shared.shape, shared.dtype),
-            jax.ShapeDtypeStruct((n,) + expert.shape[1:], expert.dtype),
+            shape((n,) + own[0].shape, bf16),
+            shape((n,) + own[1].shape, bf16),
+            shape((n,) + own[2].shape[1:], bf16),
+            shape((length, heads_width), bf16),
+            shape((length, heads_width), bf16),
+            shape((length, heads_width), bf16),
+            shape((length, heads_width), bf16),
+            shape((length, 128), f32),
+            shape((length, width), f32),
+            shape((length, width), bf16),
+            shape((length, width), bf16),
+            shape((length, 128), f32),
+            shape((length, 128), f32),
+            shape((experts, half, 2 * width), bf16),
+            shape((2, experts, half, 2 * width), bf16),
         ),
-        in_specs=[anywhere, anywhere],
-        out_specs=(anywhere, anywhere),
+        in_specs=[vmem] * len(inputs) + [anywhere] * 3,
+        out_specs=(vmem, anywhere, anywhere) + (vmem,) * 12,
         scratch_shapes=[
-            pltpu.SemaphoreType.DMA((2,)),
-            pltpu.SemaphoreType.DMA((n,)),
-            pltpu.SemaphoreType.DMA((n,)),
-            pltpu.SemaphoreType.DMA((4, n)),
-            pltpu.SemaphoreType.DMA((1 + GROUP, n)),
+            pltpu.VMEM((length, length), f32),
+            pltpu.VMEM((length, width), f32),
+            pltpu.VMEM((length, width), f32),
+            dma((3,)),
+            dma((n,)),
+            dma((4, n)),
+            dma((n,)),
+            dma((4, n)),
+            dma((n,)),
+            dma((1 + GROUP, n)),
+            dma((4,)),
+            dma((GROUP,)),
+            dma((GROUP,)),
         ],
-        compiler_params=pltpu.CompilerParams(collective_id=0, has_side_effects=True),
-    )(shared, expert)
+        compiler_params=pltpu.CompilerParams(
+            collective_id=0, has_side_effects=True, vmem_limit_bytes=48 << 20
+        ),
+    )(*inputs, *own)
 
 
 def reduce_kernel(
@@ -818,7 +1153,7 @@
     for j in range(1, GROUP):
         order = [(d, (d // GROUP) * GROUP + ((d % GROUP) ^ j)) for d in range(planes * GROUP)]
         out.append(lax.ppermute(blocks[j], "dp", order))
-    return jnp.stack(out)
+    return out
 
 
 def local_grouped(
@@ -848,83 +1183,90 @@
     heads = heads_width // HD
     scale = HD ** (-0.5)
     n = planes * GROUP
-    cuts = [2 * s_hidden, s_hidden, 3 * heads_width, heads_width, 128]
+    member = lax.rem(lax.axis_index("dp"), GROUP)
+    core = lax.axis_index("tensor")
+    cuts = [3 * heads_width, heads_width, 128, 2 * s_hidden, s_hidden]
     edges = [sum(cuts[:i]) for i in range(len(cuts) + 1)]
 
     def part(array, i):
         return array[..., edges[i] : edges[i + 1]]
 
+    expert_packed = jnp.concatenate(
+        [gate_up.reshape(experts, rows, 2 * hidden), down_weight.transpose(0, 2, 1)], axis=2
+    )
     small = jnp.concatenate([gain_attn[:, None], gain_ffn[:, None], router_weight], axis=1)
     small = jnp.pad(small, ((0, 0), (0, 128 - small.shape[1])))
-    packed = jnp.concatenate(
-        [
-            shared_gate_up.reshape(rows, 2 * s_hidden),
-            shared_down.T,
-            qkv_weight.reshape(rows, 3 * heads_width),
-            out_weight.T,
-            small,
-        ],
-        axis=1,
-    )
-    expert_packed = jnp.concatenate(
-        [gate_up.reshape(experts, rows, 2 * hidden), down_weight.transpose(0, 2, 1)], axis=2
-    )
-    all_packed, all_expert = gather_weights(planes, packed, expert_packed)
-    all_packed = all_packed.reshape(width, -1)
+    attn_packed = jnp.concatenate(
+        [qkv_weight.reshape(rows, 3 * heads_width), out_weight.T, small], axis=1
+    )
+    shared_packed = jnp.concatenate(
+        [shared_gate_up.reshape(rows, 2 * s_hidden), shared_down.T], axis=1
+    )
+    cosine, sine = rotary(length, HD)
+    cosine = jnp.tile(cosine[:, 0], (1, 4))
+    sine = jnp.tile(sine[:, 0], (1, 4))
+    orders = slot_order.reshape(length, top)
+    inputs = (
+        tokens,
+        cotangent,
+        segment_ids.reshape(length, 1),
+        segment_ids,
+        expert_ids,
+        orders,
+        expert_ids.T,
+        orders.T,
+        cosine,
+        sine,
+    )
+    (
+        all_attn,
+        all_shared,
+        all_expert,
+        queries,
+        keys_all,
+        values_all,
+        mixed,
+        log_totals,
+        hidden_state,
+        xn_one,
+        xn_two,
+        probs,
+        pair_facts,
+        _,
+        arrived,
+    ) = forward_pass(
+        planes, experts, inputs, (attn_packed, shared_packed, expert_packed), heads_width
+    )
+    all_attn = all_attn.reshape(width, -1)
+    all_shared = all_shared.reshape(width, -1)
     all_expert = all_expert.reshape(width, -1)
-    s_gate_up, s_down_t, w_qkv, w_out_t = (part(all_packed, i) for i in range(4))
-    small_all = part(all_packed, 4)
+    w_qkv, w_out_t, small_all = (part(all_attn, i) for i in range(3))
+    s_gate_up, s_down_t = all_shared[:, : 2 * s_hidden], all_shared[:, 2 * s_hidden :]
     g_one, g_two = small_all[:, 0].astype(f32), small_all[:, 1].astype(f32)
     w_router = small_all[:, 2 : 2 + experts]
     w_gate_up, w_down_t = all_expert[:, : 2 * hidden], all_expert[:, 2 * hidden :]
-
-    def mm(spec, a, b):
-        return jnp.einsum(spec, a, b, preferred_element_type=f32)
-
-    member = lax.rem(lax.axis_index("dp"), GROUP)
-    pair_expert = expert_ids.reshape(-1)
-    order = slot_order[0]
-    ahead = (pair_expert[None, :] == pair_expert[:, None]) & (order[None, :] < order[:, None])
-    position = jnp.sum(ahead.astype(jnp.int32), axis=1)
-    kept = (position < capacity).reshape(length, top)
-    slot = jnp.where(
-        kept, (jnp.bitwise_xor(pair_expert, member) * capacity + position).reshape(length, top), -1
-    )
-    kept_float = kept.astype(f32)
+    cosine, sine = rotary(length, HD)
+    half = capacity // 2
+    gates = pair_facts[:, :top]
+    slot = pair_facts[:, top : 2 * top].astype(jnp.int32)
+    kept_float = (slot >= 0).astype(f32)
+    probs = probs[:, 2 : 2 + experts]
+    match = (expert_ids[:, :, None] == jnp.arange(experts, dtype=jnp.int32)).astype(f32)
     slots = jnp.arange(experts * capacity, dtype=jnp.int32)
     pick = [(slot[:, r : r + 1] == slots[None, :]).astype(bf16) for r in range(top)]
     pick_any = sum(pick[1:], pick[0])
-
     segment = segment_ids[0]
     xfull = tokens.astype(f32)
-    rms_one = rms_scale(xfull)
-    xn_one = (xfull * rms_one * g_one).astype(bf16)
-    projected = mm("td,dc->tc", xn_one, w_qkv).reshape(length, 3, heads, HD)
-    cosine, sine = rotary(length, HD)
-    queries = rotate(projected[:, 0], cosine, sine).astype(bf16)
-    keys_all = rotate(projected[:, 1], cosine, sine).astype(bf16)
-    values_all = projected[:, 2].astype(bf16)
-    mixed, log_totals = attend_forward(queries, keys_all, values_all, segment, scale)
-    hidden_state = xfull + add_cores(mm("th,dh->td", mixed, w_out_t))
-    rms_two = rms_scale(hidden_state)
-    xn_two = (hidden_state * rms_two * g_two).astype(bf16)
-    logits = jnp.dot(xn_two, w_router, preferred_element_type=f32)
-    probs = jax.nn.softmax(logits, axis=-1)
-    match = (expert_ids[:, :, None] == jnp.arange(experts, dtype=jnp.int32)).astype(f32)
-    gates = jnp.sum(match * probs[:, None, :], axis=2) * kept_float
-
-    slot_gate = sum(
-        jnp.sum(jnp.where(slot[:, r : r + 1] == slots[None, :], gates[:, r : r + 1], 0.0), axis=0)
-        for r in range(top)
-    )
-    both = jnp.concatenate([xn_two, cotangent], axis=1)
-    placed = mm("ts,td->sd", pick_any, both)
-    placed = jnp.concatenate(
-        [placed[:, :width], placed[:, width:] * slot_gate[:, None]], axis=1
-    ).astype(bf16)
-    arrived = to_members(planes, placed.reshape(experts, capacity, 2 * width))
+    rms_one, rms_two = rms_scale(xfull), rms_scale(hidden_state)
+    queries, keys_all, values_all = (
+        a.reshape(length, heads, HD) for a in (queries, keys_all, values_all)
+    )
+    log_totals = log_totals[:, :heads].T[None]
     arrived = arrived.reshape(experts * capacity, 2 * width)
     xin, dye = arrived[:, :width], arrived[:, width:]
+
+    def mm(spec, a, b):
+        return jnp.einsum(spec, a, b, preferred_element_type=f32)
 
     shared_both = mm("td,df->tf", xn_two, s_gate_up).reshape(length, 2, s_hidden)
     shared_hidden = silu_forward(shared_both)
@@ -943,11 +1285,16 @@
     grad_in = mm("sf,df->sd", grad_both, w_gate_up).astype(bf16)
     grad_down_t = mm("sd,sf->df", dye, expert_hidden)
     grad_gate_up = mm("sd,sf->df", xin, grad_both)
-    back = jnp.concatenate([expert_out, grad_in], axis=1).reshape(experts, capacity, 2 * width)
-    back = to_members(planes, back).reshape(experts * capacity, 2 * width)
-    picked = [mm("ts,sd->td", pick[r], back[:, :width]) for r in range(top)]
+    expert_grads = jnp.concatenate([grad_gate_up.astype(bf16), grad_down_t.astype(bf16)], axis=1)
+    def home(values):
+        blocks = values.reshape(2, experts, half, width)
+        blocks = to_members(planes, [blocks[:, j] for j in range(GROUP)])
+        return jnp.stack(blocks, axis=1).reshape(experts * capacity, width)
+
+    expert_out, grad_in = home(expert_out), home(grad_in)
+    picked = [mm("ts,sd->td", pick[r], expert_out) for r in range(top)]
     moe = sum(gates[:, r : r + 1] * picked[r] for r in range(top))
-    grad_xn_moe = mm("ts,sd->td", pick_any, back[:, width:])
+    grad_xn_moe = mm("ts,sd->td", pick_any, grad_in)
     grad_y = cotangent.astype(f32)
     grad_gates_part = kept_float * jnp.stack(
         [jnp.sum(grad_y * picked[r], axis=-1) for r in range(top)], axis=1
@@ -994,27 +1341,24 @@
     shared_grads = jnp.concatenate(
         [
             g.astype(bf16)
-            for g in (grad_s_gate_up, grad_s_down_t, grad_w_qkv, grad_out_t, small_grad)
+            for g in (grad_w_qkv, grad_out_t, small_grad, grad_s_gate_up, grad_s_down_t)
         ],
         axis=1,
     ).reshape(n, rows, -1)
-    expert_grads = jnp.concatenate(
-        [grad_gate_up.astype(bf16), grad_down_t.astype(bf16)], axis=1
-    ).reshape(n, rows, -1)
-    mine, mine_expert = reduce_grads(planes, shared_grads, expert_grads)
-    small_mine = part(mine, 4)
+    mine, mine_expert = reduce_grads(planes, shared_grads, expert_grads.reshape(n, rows, -1))
+    small_mine = part(mine, 2)
     return (
         output,
         grad_tokens,
         small_mine[:, 0],
-        part(mine, 2).reshape(rows, 3, heads_width),
-        part(mine, 3).T,
+        part(mine, 0).reshape(rows, 3, heads_width),
+        part(mine, 1).T,
         small_mine[:, 1],
         small_mine[:, 2 : 2 + experts],
         mine_expert[:, :, : 2 * hidden].reshape(experts, rows, 2, hidden),
         mine_expert[:, :, 2 * hidden :].transpose(0, 2, 1),
-        part(mine, 0).reshape(rows, 2, s_hidden),
-        part(mine, 1).T,
+        part(mine, 3).reshape(rows, 2, s_hidden),
+        part(mine, 4).T,
     )
 
 

time: 467 us -> 465 us (level); the launches traced: 458 us -> 461 us
  waiting for transfers between devices: 41 us -> 3.79 us
  Pallas kernels: 269 us -> 294 us
  other arithmetic: 24.4 us -> 37.1 us
  local copies, waits for them, and re-layouts: 32.7 us -> 39.1 us
    ppermute x6, waiting for transfers between devices: 40.3 us -> 3.78 us  [to_members(): out.append(lax.ppermute(blocks[j], 'dp', order))]
    pallas_call x1, Pallas kernels: 160 us -> 173 us  [reduce_grads(): pl.pallas_call(functools.partial(reduce_kernel, planes), out_shape=(jax.S...]
    pallas_call x1, Pallas kernels: 109 us -> 121 us  [forward_pass(): pl.pallas_call(functools.partial(forward_kernel, planes, experts), out_sh...]
    dot_general x22 -> x19, matrix products: 63.1 us -> 53.9 us  [mm(): return jnp.einsum(spec, a, b, preferred_element_type=f32)]
    reshape x1, matrix products: 3.6 us -> 9.78 us  [local_grouped(): both_parts = mm('sd,df->sf', xin, w_gate_up).reshape(-1, 2, hidden)]
  transfers between devices with their start and end apart: 11 -> 10, of which waited for: 4 -> 1; matrix products, arithmetic and copies ran while one was open for 9% -> 15% of each run, Pallas kernels for 0% -> 0%
where the time goes in v2:
time: 465 us; the launch traced here: 461 us
  Pallas kernels  294 us (63%)
  matrix products  77.6 us (17%)
  local copies, waits for them, and re-layouts  39.1 us (8%)
  other arithmetic  37.1 us (8%)
  starting transfers between devices  8.19 us (2%)
    pallas_call x1, Pallas kernels, reduce_grads(): pl.pallas_call(functools.partial(reduce_kernel, planes), out_shape=(jax.S...  173 us
    pallas_call x1, Pallas kernels, forward_pass(): pl.pallas_call(functools.partial(forward_kernel, planes, experts), out_sh...  121 us
    dot_general x19, matrix products, mm(): return jnp.einsum(spec, a, b, preferred_element_type=f32)  53.9 us
    reshape x1, matrix products, local_grouped(): both_parts = mm('sd,df->sf', xin, w_gate_up).reshape(-1, 2, hidden)  9.78 us
  transfers between devices with their start and end apart: 10, of which 1 were waited for; matrix products, arithmetic and copies ran while one was open for 15% of the time, Pallas kernels for 0%

profile of v2, /device:TPU:8, one launch (start us, length us, event | category | flops | bytes accessed | tf_op | source)
XLA Modules:
  0.0 461.5 jit_solution(16587634377816563615)
XLA Ops:
  0.7 0.9 fusion.77
  3.1 1.3 reduce.19
  4.8 2.5 reshape.327
  7.9 1.1 pad_maximum_fusion.5.e_own
  9.1 120.5 %shard_map.224 = (bf16[16,48,1664]{2,1,0:T(8,128)(2,1)}, bf16[16,48,3072]{2,1,0:T(8,128)(2,1)}, bf16[16,48,3072]{2,1,0:T(8,128)(2,1)}, bf16[512,384]{1,0:T(8,128...) custom-call(bf16[512,768]{1,0:T(8,128)(2,1)} %x_ref.1, ...), custom_call_target="tpu_custom_call" | custom-call | tf_op jit(solution)/shard_map/pallas_call | solution.py:881
  129.6 9.8 %fusion.12 = f32[1024,2048]{0,1:T(8,128)} fusion(bf16[768,3072]{1,0:T(8,128)(2,1)} %bitcast.237, bf16[1024,1536]{1,0:T(8,128)(2,1)} %bitcast.241), kind=kOutput, calls=%fused_computation.25 | convolution fusion | flops 3221225472 | bytes 13107200 | tf_op jit(solution)/shard_map/reshape | solution.py:1280
  139.5 5.9 %fusion.23 = (bf16[1024,1,1024]{0,2,1:T(8,128)(2,1)S(1)}, bf16[1024,1,1024]{0,2,1:T(8,128)(2,1)S(1)}, bf16[1024,1024]{0,1:T(8,128)(2,1)S(1)}) fusion(f32[1024,2,1024]{0,2,1:T(8,128)} %bitcast.245, bf16[768,3072]{1,0:T(8,128)(2,1)S(1)} %bitcast.238, bf16[1024,1536]{1,0:T(8,128)(2,1)S(1)} %bitcast.242), kind=kOutput, calls=%fused_computation.52 | convolution fusion | flops 1627389952 | bytes 17825792 | tf_op jit(solution)/shard_map/sd,df->sf/dot_general | solution.py:1269
  145.4 1.9 convolution_convert_fusion.5
  147.3 1.2 fusion.82
  148.4 1.5 collective-permute-start
  150.5 1.5 collective-permute-start.2
  152.3 3.5 fusion.26
  155.9 1.2 fusion.81
  157.0 1.5 collective-permute-start.4
  159.0 5.0 %convolution_convert_fusion.1 = bf16[768,2048]{1,0:T(8,128)(2,1)} fusion(bf16[1024,2048]{0,1:T(8,128)(2,1)S(1)} %bitcast.194, bf16[1024,1536]{1,0:T(8,128)(2,1)S(1)} %bitcast.243), kind=kOutput, calls=%fused_computation.12 | convolution fusion | flops 3222798336 | bytes 8912896 | tf_op jit(solution)/shard_map/sd,sf->df/dot_general | solution.py:1269
  164.1 3.0 convolution_convert_fusion.4
  167.2 0.9 slice_reduce_fusion.3
  169.7 1.9 fusion.8
  171.6 2.8 fusion.69
  174.7 3.0 fusion.6
  177.7 1.8 fusion.80
  179.7 1.6 multiply_reduce_fusion.3
  183.1 0.9 copy.188
  184.0 0.9 fusion.67
  184.9 1.0 copy.211
  186.0 1.3 multiply_multiply_fusion
  187.3 4.9 %pad_maximum_fusion = bf16[768,3072]{1,0:T(8,128)(2,1)} fusion(bf16[768,1024]{1,0:T(8,128)(2,1)} %convolution_convert_fusion.4, bf16[768,2048]{1,0:T(8,128)(2,1)} %convolution_convert_fusion.1), kind=kLoop, calls=%fused_computation.3 | loop fusion | flops 9437184 | bytes 9437184 | tf_op jit(solution)/shard_map/concatenate | solution.py:1288
  192.2 3.7 fusion.89
  195.9 1.5 collective-permute-start.6
  197.4 1.4 pad_maximum_fusion.3
  198.9 1.5 fusion.19
  200.4 2.3 fusion.29
  202.8 3.8 collective-permute-done.6
  206.6 1.3 pad_maximum_fusion.4
  207.9 2.4 convolution_add_fusion
  211.2 4.7 %add_convert_fusion.1 = bf16[512,768]{1,0:T(8,128)(2,1)} fusion(f32[512,768]{1,0:T(8,128)} %copy-done.55, f32[512,768]{1,0:T(8,128)} %get-tuple-element.175, bf16[512,1024]{0,1:T(8,128)(2,1)} %get-tuple-element.149, bf16[768,3072]{1,0:T(8,128)(2,1)} %bitcast.231, f32[512]{0:T(512)S(1)} %copy-done.47, f32[512]{0:T(512)S(1)} %copy-done.46), kind=kOutput, calls=%fused_computation.77 | convolution fusion | flops 807272448 | bytes 6557696 | tf_op jit(solution)/shard_map/tf,df->td/dot_general | solution.py:1269
  216.7 1.2 copy.181
  218.8 1.2 multiply_reduce_fusion.4
  220.8 1.1 multiply_convert_fusion.5
  221.9 1.4 fusion.74
  223.3 2.7 multiply_reduce_fusion.1
  226.1 3.0 convert_add_fusion
  229.1 2.1 convolution_convert_fusion.7
  231.3 4.8 %multiply_reduce_fusion = (f32[6,512]{1,0:T(8,128)S(1)}, f32[6,512,512]{1,2,0:T(8,128)}) fusion(f32[6,512,512]{1,2,0:T(8,128)S(1)} %bitcast.191, f32[6,512]{1,0:T(8,128)S(1)} %copy-done.38, pred[512,512]{0,1:T(8,128)(4,1)S(1)} %copy-done.23, bf16[512,6,64]{0,2,1:T(8,128)(2,1)S(1)} %bitcast.206, bf16[512,6,64]{0,2,1:T(8,128)(2,1)S(1)} %bitcast.208), kind=kOutput, calls=%fused_computation.1 | convolution fusion | flops 209187840 | bytes 13656064 | tf_op jit(solution)/shard_map/while/body/eval_jaxpr/qhd,khd->hqk/dot_general | solution.py:136
  236.1 4.7 %multiply_convert_fusion = bf16[6,512,512]{1,2,0:T(8,128)(2,1)S(1)} fusion(f32[6,512,512]{1,2,0:T(8,128)} %get-tuple-element.177, f32[6,512,512]{1,2,0:T(8,128)S(1)} %bitcast.191, f32[6,512]{1,0:T(8,128)S(1)} %get-tuple-element.176, f32[6,512]{1,0:T(8,128)S(1)} %copy-done.38, pred[512,512]{0,1:T(8,128)(4,1)S(1)} %copy-done.23), kind=kLoop, calls=%fused_computation | loop fusion | flops 9437184 | bytes 16015360 | tf_op jit(solution)/shard_map/while/body/eval_jaxpr/convert_element_type | solution.py:140
  240.8 1.1 fusion.52
  242.6 1.9 fusion.57
  245.0 1.9 copy-done.33
  246.9 1.3 fusion.39
  249.1 1.3 convolution_convert_fusion.6
  250.4 2.1 copy.194
  252.6 3.9 fusion
  256.5 1.0 constant_dynamic-update-slice_fusion
  257.5 2.5 fusion.37
  260.9 5.3 %fusion.1 = bf16[768,4736]{1,0:T(8,128)(2,1)} fusion(bf16[768,4736]{1,0:T(8,128)(2,1)} %pad_dynamic-update-slice_fusion, bf16[512,768]{1,0:T(8,128)(2,1)S(1)} %get-tuple-element.64, bf16[512,2048]{0,1:T(8,128)(2,1)} %bitcast.200), kind=kOutput, calls=%fused_computation.15 | convolution fusion | flops 1612185600 | bytes 6029312 | tf_op jit(solution)/shard_map/td,tf->df/dot_general | solution.py:1269
  266.2 2.3 bitcast_dynamic-update-slice_fusion
  268.4 173.3 %shard_map.225 = (f32[48,4736]{1,0:T(8,128)}, f32[4,48,3072]{2,1,0:T(8,128)}) custom-call(bf16[16,48,4736]{2,1,0:T(8,128)(2,1)} %bitcast.57.s_ref, bf16[16,48,3072]{2,1,0:T(8,128)(2,1)} %bitcast.192), custom_call_target="tpu_custom_call" | custom-call | tf_op jit(solution)/shard_map/pallas_call | solution.py:1110
  441.7 2.8 slice.183
  444.6 2.1 slice_bitcast_fusion.4
  450.1 3.6 reshape.343
  453.7 1.1 reshape.344
  454.7 1.6 copy.217
  456.4 1.4 copy.197
  458.4 2.8 fusion.34
  (196 shorter events, 18.1 us)
Async XLA Ops:
  0.6 6.7 %copy-start.37 = (bf16[48,2,1024]{2,1,0:T(2,128)(2,1)S(1)}, bf16[48,2,1024]{2,1,0:T(2,128)(2,1)}, u32[]{:S(2)}) copy-start(bf16[48,2,1024]{2,1,0:T(2,128)(2,1)} %param.25) | copy-start | bytes 589828
  1.6 5.8 %copy-start.39 = (bf16[48,3,384]{2,0,1:T(8,128)(2,1)S(1)}, bf16[48,3,384]{2,0,1:T(8,128)(2,1)}, u32[]{:S(2)}) copy-start(bf16[48,3,384]{2,0,1:T(8,128)(2,1)} %param.19) | copy-start | bytes 331780
  2.3 5.2 %copy-start.50 = (bf16[48,4]{0,1:T(4,128)(2,1)S(1)}, bf16[48,4]{0,1:T(4,128)(2,1)}, u32[]{:S(2)}) copy-start(bf16[48,4]{0,1:T(4,128)(2,1)} %param.22) | copy-start | bytes 1156
  2.3 5.2 %copy-start.51 = (bf16[48]{0:T(256)(128)(2,1)S(1)}, bf16[48]{0:T(256)(128)(2,1)}, u32[]{:S(2)}) copy-start(bf16[48]{0:T(256)(128)(2,1)} %param.21) | copy-start | bytes 292
  2.3 5.2 %copy-start.52 = (bf16[48]{0:T(256)(128)(2,1)S(1)}, bf16[48]{0:T(256)(128)(2,1)}, u32[]{:S(2)}) copy-start(bf16[48]{0:T(256)(128)(2,1)} %param.18) | copy-start | bytes 292
  2.3 5.3 %copy-start.7 = (s32[1,512]{1,0:T(1,128)S(1)}, s32[1,512]{1,0:T(1,128)}, u32[]{:S(2)}) copy-start(s32[1,512]{1,0:T(1,128)} %seg_row.1) | copy-start | bytes 6148
  2.3 5.5 %copy-start.6 = (s32[512,2]{0,1:T(2,128)S(1)}, s32[512,2]{0,1:T(2,128)}, u32[]{:S(2)}) copy-start(s32[512,2]{0,1:T(2,128)} %param.16) | copy-start | bytes 12292
  2.4 5.5 %copy-start.34 = (bf16[4,1024,48]{1,2,0:T(8,128)(2,1)S(1)}, bf16[4,1024,48]{1,2,0:T(8,128)(2,1)}, u32[]{:S(2)}) copy-start(bf16[4,1024,48]{1,2,0:T(8,128)(2,1)} %param.24) | copy-start | bytes 1179652
  129.6 9.8 %copy-start = (bf16[512,384]{1,0:T(8,128)(2,1)}, bf16[512,384]{1,0:T(8,128)(2,1)S(1)}, u32[]{:S(2)}) copy-start(bf16[512,384]{1,0:T(8,128)(2,1)S(1)} %get-tuple-element.69) | copy-start | bytes 1179652
  129.6 9.8 %copy-start.2 = (bf16[512,384]{1,0:T(8,128)(2,1)}, bf16[512,384]{1,0:T(8,128)(2,1)S(1)}, u32[]{:S(2)}) copy-start(bf16[512,384]{1,0:T(8,128)(2,1)S(1)} %get-tuple-element.68) | copy-start | bytes 1179652
  129.6 9.8 %copy-start.4 = (f32[512,128]{1,0:T(8,128)}, f32[512,128]{1,0:T(8,128)S(1)}, u32[]{:S(2)}) copy-start(f32[512,128]{1,0:T(8,128)S(1)} %get-tuple-element.70) | copy-start | bytes 786436
  129.6 9.8 %copy-start.8 = (bf16[512,768]{1,0:T(8,128)(2,1)}, bf16[512,768]{1,0:T(8,128)(2,1)S(1)}, u32[]{:S(2)}) copy-start(bf16[512,768]{1,0:T(8,128)(2,1)S(1)} %get-tuple-element.72) | copy-start | bytes 2359300
  129.6 9.8 %copy-start.53 = (bf16[16,48,3072]{2,1,0:T(8,128)(2,1)S(1)}, bf16[16,48,3072]{2,1,0:T(8,128)(2,1)}, u32[]{:S(2)}) copy-start(bf16[16,48,3072]{2,1,0:T(8,128)(2,1)} %get-tuple-element.63) | copy-start | bytes 14155780
  129.6 9.8 %copy-start.54 = (bf16[2,4,128,1536]{3,2,1,0:T(8,128)(2,1)S(1)}, bf16[2,4,128,1536]{3,2,1,0:T(8,128)(2,1)}, u32[]{:S(2)}) copy-start(bf16[2,4,128,1536]{3,2,1,0:T(8,128)(2,1)} %get-tuple-element.62) | copy-start | bytes 9437188
  148.4 47.4 %collective-permute-start = (bf16[2,128,768]{2,1,0:T(8,128)(2,1)}, bf16[2,128,768]{2,1,0:T(8,128)(2,1)}, u32[]{:S(2)}, u32[]{:S(2)}) collective-permute-start(bf16[2,128,768]{2,1,0:T(8,128)(2,1)} %get-tuple-element.160), channel_id=1, source_target_pairs={{0,2},{2,0},{4,6},{6,4},{8,10},{10,8},{12,14},{14,12},{16,18},{18,... | collective-permute-start | bytes 1179656 | tf_op jit(solution)/shard_map/ppermute | solution.py:1155
  150.0 47.4 %collective-permute-start.1 = (bf16[2,128,768]{2,1,0:T(8,128)(2,1)}, bf16[2,128,768]{2,1,0:T(8,128)(2,1)}, u32[]{:S(2)}, u32[]{:S(2)}) collective-permute-start(bf16[2,128,768]{2,1,0:T(8,128)(2,1)} %get-tuple-element.159), channel_id=1, source_target_pairs={{0,4},{2,6},{4,0},{6,2},{8,12},{10,14},{12,8},{14,10},{16,20},{18,... | collective-permute-start | bytes 1179656 | tf_op jit(solution)/shard_map/ppermute | solution.py:1155
  150.5 46.9 %collective-permute-start.2 = (bf16[2,128,768]{2,1,0:T(8,128)(2,1)}, bf16[2,128,768]{2,1,0:T(8,128)(2,1)}, u32[]{:S(2)}, u32[]{:S(2)}) collective-permute-start(bf16[2,128,768]{2,1,0:T(8,128)(2,1)} %get-tuple-element.161), channel_id=1, source_target_pairs={{0,6},{2,4},{4,2},{6,0},{8,14},{10,12},{12,10},{14,8},{16,22},{18,... | collective-permute-start | bytes 1179656 | tf_op jit(solution)/shard_map/ppermute | solution.py:1155
  155.9 13.9 %slice-start.2 = ((s8[4718592]{0:T(1024)(128)(4,1)}), s8[4194304]{0:T(1024)(128)(4,1)S(1)}, s32[]{:S(2)}) async-start(s8[4718592]{0:T(1024)(128)(4,1)} %bitcast.232), calls=%async_computation.2 | async-start | bytes 8388608
  157.0 45.7 %collective-permute-start.4 = (bf16[2,128,768]{2,1,0:T(8,128)(2,1)}, bf16[2,128,768]{2,1,0:T(8,128)(2,1)}, u32[]{:S(2)}, u32[]{:S(2)}) collective-permute-start(bf16[2,128,768]{2,1,0:T(8,128)(2,1)} %get-tuple-element.156), channel_id=1, source_target_pairs={{0,2},{2,0},{4,6},{6,4},{8,10},{10,8},{12,14},{14,12},{16,18},{18,... | collective-permute-start | bytes 1179656 | tf_op jit(solution)/shard_map/ppermute | solution.py:1155
  158.5 11.2 %slice-start.3 = ((s8[4718592]{0:T(1024)(128)(4,1)}), s8[524288]{0:T(1024)(128)(4,1)S(1)}, s32[]{:S(2)}) async-start(s8[4718592]{0:T(1024)(128)(4,1)} %bitcast.232), calls=%async_computation.3 | async-start | bytes 1048576
  158.5 44.2 %collective-permute-start.5 = (bf16[2,128,768]{2,1,0:T(8,128)(2,1)}, bf16[2,128,768]{2,1,0:T(8,128)(2,1)}, u32[]{:S(2)}, u32[]{:S(2)}) collective-permute-start(bf16[2,128,768]{2,1,0:T(8,128)(2,1)} %get-tuple-element.155), channel_id=1, source_target_pairs={{0,4},{2,6},{4,0},{6,2},{8,12},{10,14},{12,8},{14,10},{16,20},{18,... | collective-permute-start | bytes 1179656 | tf_op jit(solution)/shard_map/ppermute | solution.py:1155
  164.1 4.0 copy-start.13
  174.7 3.0 copy-start.25
  177.7 4.2 copy-start.3
  177.7 4.4 copy-start.1
  177.7 4.6 %copy-start.5 = (f32[512,128]{1,0:T(8,128)S(1)}, f32[512,128]{1,0:T(8,128)}, u32[]{:S(2)}) copy-start(f32[512,128]{1,0:T(8,128)} %copy-done.4) | copy-start | bytes 786436
  182.3 9.8 %copy-start.15 = (bf16[512,384]{0,1:T(8,128)(2,1)}, bf16[512,384]{0,1:T(8,128)(2,1)S(1)}, u32[]{:S(2)}) copy-start(bf16[512,384]{0,1:T(8,128)(2,1)S(1)} %copy.186) | copy-start | bytes 1179652
  192.2 3.7 copy-start.35
  192.2 5.2 %copy-start.27 = (bf16[2,1,128,768]{3,2,1,0:T(8,128)(2,1)S(1)}, bf16[2,1,128,768]{3,2,1,0:T(8,128)(2,1)}, u32[]{:S(2)}) copy-start(bf16[2,1,128,768]{3,2,1,0:T(8,128)(2,1)} %get-tuple-element.158) | copy-start | bytes 1179652
  195.8 3.0 copy-start.49
  195.9 10.7 %collective-permute-start.6 = (bf16[2,128,768]{2,1,0:T(8,128)(2,1)S(1)}, bf16[2,128,768]{2,1,0:T(8,128)(2,1)S(1)}, u32[]{:S(2)}, u32[]{:S(2)}) collective-permute-start(bf16[2,128,768]{2,1,0:T(8,128)(2,1)S(1)} %copy-done.35), channel_id=1, source_target_pairs={{0,6},{2,4},{4,2},{6,0},{8,14},{10,12},{12,10},{14,8},{16,22},{18,... | collective-permute-start | bytes 1179656 | tf_op jit(solution)/shard_map/ppermute | solution.py:1155
  200.4 2.4 copy-start.55
  200.4 6.2 %copy-start.26 = (bf16[2,1,128,768]{3,2,1,0:T(8,128)(2,1)S(1)}, bf16[2,1,128,768]{3,2,1,0:T(8,128)(2,1)}, u32[]{:S(2)}) copy-start(bf16[2,1,128,768]{3,2,1,0:T(8,128)(2,1)} %get-tuple-element.154) | copy-start | bytes 1179652
  202.8 5.1 %copy-start.57 = (f32[512,768]{1,0:T(8,128)S(1)}, f32[512,768]{1,0:T(8,128)}, u32[]{:S(2)}) copy-start(f32[512,768]{1,0:T(8,128)} %fusion.6) | copy-start | bytes 4718596
  207.9 3.3 copy-start.46
  207.9 3.3 copy-start.47
  210.3 13.0 %collective-permute-start.7 = (f32[512,768]{1,0:T(8,128)}, f32[512,768]{1,0:T(8,128)}, u32[]{:S(2)}, u32[]{:S(2)}) collective-permute-start(f32[512,768]{1,0:T(8,128)} %convolution_add_fusion), channel_id=1, source_target_pairs={{0,1},{1,0},{2,3},{3,2},{4,5},{5,4},{6,7},{7,6},{8,9},{9,8},{10,11... | collective-permute-start | bytes 4718600 | tf_op jit(solution)/shard_map/ppermute | solution.py:1144
  210.6 5.3 %collective-permute-start.8 = (f32[512,2]{1,0:T(8,128)S(1)}, f32[512,2]{1,0:T(8,128)S(1)}, u32[]{:S(2)}, u32[]{:S(2)}) collective-permute-start(f32[512,2]{1,0:T(8,128)S(1)} %compare_select_fusion), channel_id=1, source_target_pairs={{0,1},{1,0},{2,3},{3,2},{4,5},{5,4},{6,7},{7,6},{8,9},{9,8},{10,11... | collective-permute-start | bytes 12296 | tf_op jit(solution)/shard_map/ppermute | solution.py:1144
  215.9 10.1 %collective-permute-start.3 = (bf16[512,768]{1,0:T(8,128)(2,1)}, bf16[512,768]{1,0:T(8,128)(2,1)}, u32[]{:S(2)}, u32[]{:S(2)}) collective-permute-start(bf16[512,768]{1,0:T(8,128)(2,1)} %add_convert_fusion.1), channel_id=1, source_target_pairs={{0,1},{1,0},{2,3},{3,2},{4,5},{5,4},{6,7},{7,6},{8,9},{9,8},{10,11... | collective-permute-start | bytes 2359304 | tf_op jit(solution)/shard_map/ppermute | solution.py:1144
  216.7 6.6 %copy-start.12 = (f32[512,768]{1,0:T(8,128)S(1)}, f32[512,768]{1,0:T(8,128)}, u32[]{:S(2)}) copy-start(f32[512,768]{1,0:T(8,128)} %get-tuple-element.60) | copy-start | bytes 4718596
  216.7 6.6 %copy-start.43 = (f32[512]{0:T(512)S(1)}, f32[512]{0:T(512)}, u32[]{:S(2)}) copy-start(f32[512]{0:T(512)} %get-tuple-element.174) | copy-start | bytes 6148
  223.3 2.8 copy-start.19
  223.3 2.8 copy-start.45
  223.3 7.9 %slice-start = ((s8[6291456]{0:T(1024)(128)(4,1)}), s8[4194304]{0:T(1024)(128)(4,1)S(1)}, s32[]{:S(2)}) async-start(s8[6291456]{0:T(1024)(128)(4,1)} %bitcast.190), calls=%async_computation | async-start | bytes 8388608
  226.1 5.2 %slice-start.1 = ((s8[6291456]{0:T(1024)(128)(4,1)}), s8[2097152]{0:T(1024)(128)(4,1)S(1)}, s32[]{:S(2)}) async-start(s8[6291456]{0:T(1024)(128)(4,1)} %bitcast.190), calls=%async_computation.1 | async-start | bytes 4194304
  229.1 19.9 %copy-start.10 = (f32[512,768]{1,0:T(8,128)}, f32[512,768]{1,0:T(8,128)S(1)}, u32[]{:S(2)}) copy-start(f32[512,768]{1,0:T(8,128)S(1)} %get-tuple-element.152) | copy-start | bytes 4718596
  229.1 2.1 copy-start.23
  229.1 2.2 copy-start.28
  229.1 2.2 copy-start.38
  236.1 4.7 %copy-start.16 = (bf16[512,384]{0,1:T(8,128)(2,1)S(1)}, bf16[512,384]{0,1:T(8,128)(2,1)}, u32[]{:S(2)}) copy-start(bf16[512,384]{0,1:T(8,128)(2,1)} %copy-done.15) | copy-start | bytes 1179652
  244.8 2.1 copy-start.33
  245.0 3.2 copy-start.29
  248.2 9.2 %copy-start.21 = (bf16[512,768]{1,0:T(8,128)(2,1)}, bf16[512,768]{1,0:T(8,128)(2,1)S(1)}, u32[]{:S(2)}) copy-start(bf16[512,768]{1,0:T(8,128)(2,1)S(1)} %fusion.39) | copy-start | bytes 2359300
  248.2 9.2 %collective-permute-start.9 = (bf16[512,768]{1,0:T(8,128)(2,1)S(1)}, bf16[512,768]{1,0:T(8,128)(2,1)}, u32[]{:S(2)}, u32[]{:S(2)}) collective-permute-start(bf16[512,768]{1,0:T(8,128)(2,1)S(1)} %fusion.39), channel_id=1, source_target_pairs={{0,1},{1,0},{2,3},{3,2},{4,5},{5,4},{6,7},{7,6},{8,9},{9,8},{10,11... | collective-permute-start | bytes 2359304 | tf_op jit(solution)/shard_map/ppermute | solution.py:1144
  249.0 3.6 copy-start.9
  252.6 3.9 copy-start.24
  252.6 4.9 %copy-start.14 = (bf16[512,768]{1,0:T(8,128)(2,1)S(1)}, bf16[512,768]{1,0:T(8,128)(2,1)}, u32[]{:S(2)}) copy-start(bf16[512,768]{1,0:T(8,128)(2,1)} %x_ref.1) | copy-start | bytes 2359300
  252.6 4.9 %copy-start.42 = (f32[512]{0:T(512)S(1)}, f32[512]{0:T(512)}, u32[]{:S(2)}) copy-start(f32[512]{0:T(512)} %get-tuple-element.172) | copy-start | bytes 6148
  260.9 5.3 %copy-start.20 = (bf16[512,768]{1,0:T(8,128)(2,1)S(1)}, bf16[512,768]{1,0:T(8,128)(2,1)}, u32[]{:S(2)}) copy-start(bf16[512,768]{1,0:T(8,128)(2,1)} %cot_ref.1) | copy-start | bytes 2359300
  260.9 5.3 %copy-start.56 = (bf16[512,1024]{0,1:T(8,128)(2,1)S(1)}, bf16[512,1024]{0,1:T(8,128)(2,1)}, u32[]{:S(2)}) copy-start(bf16[512,1024]{0,1:T(8,128)(2,1)} %get-tuple-element.149) | copy-start | bytes 3145732
  441.7 4.9 %copy-start.30 = (f32[48,4736]{1,0:T(8,128)S(1)}, f32[48,4736]{1,0:T(8,128)}, u32[]{:S(2)}) copy-start(f32[48,4736]{1,0:T(8,128)} %get-tuple-element.74) | copy-start | bytes 2727940
  450.1 8.3 %copy-start.11 = (f32[512,768]{1,0:T(8,128)S(1)}, f32[512,768]{1,0:T(8,128)}, u32[]{:S(2)}) copy-start(f32[512,768]{1,0:T(8,128)} %copy-done.10) | copy-start | bytes 4718596
  450.1 8.3 %copy-start.22 = (bf16[512,768]{1,0:T(8,128)(2,1)S(1)}, bf16[512,768]{1,0:T(8,128)(2,1)}, u32[]{:S(2)}) copy-start(bf16[512,768]{1,0:T(8,128)(2,1)} %copy-done.21) | copy-start | bytes 2359300
  450.1 8.3 %copy-start.44 = (f32[512]{0:T(512)S(1)}, f32[512]{0:T(512)}, u32[]{:S(2)}) copy-start(f32[512]{0:T(512)} %get-tuple-element.171) | copy-start | bytes 6148
  (8 other events, 13.0 us)
